TPU v7x, 32 devices: a whole 2x2x4 slice. The times are simulated.
32 devices in a mesh: section: 4 (over y, core), batch: 8 (over z, x).
Axes of the slice: x: 2, y: 2, z: 4, core: 2. Of those that a mesh axis runs over, the one named last changes fastest.
Arguments:
- inputs: bfloat16 [16, 256, 1024], P('batch'), may hold values from -6 to 6
- segments: int32 [16, 256], P('batch'), may hold values from 0 to 5, never falling along the last dimension, each value on 1 to 128 neighbouring positions
- timestep: int32 [16], P('batch'), may hold values from 0 to 4999
- weight_in: bfloat16 [4, 1024, 4096], P('section', 'batch'), as said below
- weight_out: bfloat16 [4, 4096, 1024], P('section', 'batch'), may hold values from -0.125 to 0.125
- vectors: bfloat16 [4, 7, 1024], P('section', None, 'batch'), as said below
- cotangent: bfloat16 [16, 256, 1024], P('batch'), may hold values from -6 to 6
Outputs:
- output: bfloat16 [16, 256, 1024], P('batch', 'section')
- input_grad: float32 [16, 256, 1024], P('batch', 'section')
- weight_in_grad: float32 [4, 1024, 4096], P('section', 'batch')
- weight_out_grad: float32 [4, 4096, 1024], P('section', 'batch')
- vectors_grad: float32 [4, 7, 1024], P('section', None, 'batch')
Inputs may be any that keep to these rules, and one draw needn't show every extreme that they name: `segments`: segment numbers never fall along a sequence; a token attends only to tokens of its own sequence with the same segment number. `weight_in`: entries lie within 16 / sqrt(1024) of zero. `vectors`: entries lie within -4 and 4.
All inputs are finite; a program needn't handle non-finite values.
Results may differ from a plain program's by a relative error of at most 0.025.
Values may be sent and summed in bfloat16 or wider, within the bound.
No kernel may reach another device: no remote copies, remote signals or barrier semaphores. Data moves between devices by JAX's collectives and lax.ppermute only.
A program may use at most 192 MiB of HBM per device.

v0:
```python
import math

import jax
import jax.numpy as jnp
from jax import lax
from jax.sharding import PartitionSpec as P

FF = 4096
HEADS = 16
HEAD_DIM = 64
MICRO = 2
MB_SEQS = 1
STEPS = 5000


norm_eps = 1e-05
masked_score = -1e30


def as_sent(value):
    return jax.tree.map(lambda a: a.astype(jnp.bfloat16) if a.dtype == jnp.float32 else a, value)


def shifted(block, axis, distance):
    devices = range(lax.axis_size(axis))
    route = [(i - distance, i) for i in devices if i - distance in devices]
    return lax.ppermute(block, axis, route)


def contract_rows(first_operand, second_operand):
    return lax.dot_general(
        first_operand, second_operand, (((0,), (0,)), ((), ())), preferred_element_type=jnp.float32
    )


def contract_cols(first_operand, second_operand):
    return lax.dot_general(
        first_operand, second_operand, (((1,), (1,)), ((), ())), preferred_element_type=jnp.float32
    )


def layer_norm(resid, ln_gain, ln_shift):
    average = jnp.mean(resid, axis=-1, keepdims=True)
    centred = resid - average
    variance = jnp.mean(centred * centred, axis=-1, keepdims=True)
    return centred * lax.rsqrt(variance + norm_eps) * ln_gain + ln_shift


def norm_backward(grad_out, resid, ln_gain):
    average = jnp.mean(resid, axis=-1, keepdims=True)
    centred = resid - average
    variance = jnp.mean(centred * centred, axis=-1, keepdims=True)
    inverse = lax.rsqrt(variance + norm_eps)
    normed = centred * inverse
    gain_grad = jnp.sum(grad_out * normed, axis=0)
    shift_grad = jnp.sum(grad_out, axis=0)
    normed_grad = grad_out * ln_gain
    grad_resid = inverse * (
        normed_grad
        - jnp.mean(normed_grad, axis=-1, keepdims=True)
        - normed * jnp.mean(normed_grad * normed, axis=-1, keepdims=True)
    )
    return (grad_resid, gain_grad, shift_grad)


def gelu_slope(upper):
    cumulative = 0.5 * (1.0 + lax.erf(upper * (1.0 / math.sqrt(2.0))))
    density = jnp.exp(-0.5 * upper * upper) * (1.0 / math.sqrt(2.0 * math.pi))
    return cumulative + upper * density


def attention_core(query, key_rows, value_rows, seg_rows):
    seq_count, length, width = query.shape
    block_rows = min(512, length)
    blocks = length // block_rows
    factor = 1.0 / math.sqrt(HEAD_DIM)

    def one_sequence(items):
        query_seq, key_seq, value_seq, seg_seq = items
        key_heads = key_seq.reshape(length, HEADS, HEAD_DIM)
        value_heads = value_seq.reshape(length, HEADS, HEAD_DIM)

        def one_block(carried, block_index):
            query_block = lax.dynamic_slice_in_dim(
                query_seq, block_index * block_rows, block_rows, 0
            ).reshape(block_rows, HEADS, HEAD_DIM)
            seg_block = lax.dynamic_slice_in_dim(seg_seq, block_index * block_rows, block_rows, 0)
            scores = (
                jnp.einsum(
                    "qhe,khe->hqk", query_block, key_heads, preferred_element_type=jnp.float32
                )
                * factor
            )
            allowed = (seg_block[:, None] == seg_seq[None, :])[None]
            scores = jnp.where(allowed, scores, masked_score)
            peaks = jnp.max(scores, axis=2, keepdims=True)
            exponent = jnp.exp(scores - peaks)
            totals = jnp.sum(exponent, axis=2, keepdims=True)
            weights_low = (exponent / totals).astype(jnp.bfloat16)
            context = jnp.einsum(
                "hqk,khe->qhe", weights_low, value_heads, preferred_element_type=jnp.float32
            )
            return (
                carried,
                (context.reshape(block_rows, width), (peaks + jnp.log(totals))[:, :, 0]),
            )

        unused, (contexts, log_totals) = lax.scan(one_block, 0, jnp.arange(blocks))
        return (contexts.reshape(length, width), log_totals)

    return lax.map(one_sequence, (query, key_rows, value_rows, seg_rows))


def attention_core_back(query, key_rows, value_rows, seg_rows, log_totals, grad_context):
    seq_count, length, width = query.shape
    block_rows = min(512, length)
    blocks = length // block_rows
    factor = 1.0 / math.sqrt(HEAD_DIM)

    def one_sequence(items):
        query_seq, key_seq, value_seq, seg_seq, totals_seq, grad_seq = items
        key_heads = key_seq.reshape(length, HEADS, HEAD_DIM)
        value_heads = value_seq.reshape(length, HEADS, HEAD_DIM)

        def one_block(carried, block_index):
            key_grad_acc, value_grad_acc = carried
            query_block = lax.dynamic_slice_in_dim(
                query_seq, block_index * block_rows, block_rows, 0
            ).reshape(block_rows, HEADS, HEAD_DIM)
            grad_block = lax.dynamic_slice_in_dim(
                grad_seq, block_index * block_rows, block_rows, 0
            ).reshape(block_rows, HEADS, HEAD_DIM)
            seg_block = lax.dynamic_slice_in_dim(seg_seq, block_index * block_rows, block_rows, 0)
            block_totals = lax.dynamic_index_in_dim(totals_seq, block_index, 0, keepdims=False)
            scores = (
                jnp.einsum(
                    "qhe,khe->hqk", query_block, key_heads, preferred_element_type=jnp.float32
                )
                * factor
            )
            allowed = (seg_block[:, None] == seg_seq[None, :])[None]
            probs = jnp.where(allowed, jnp.exp(scores - block_totals[:, :, None]), 0.0)
            probs_low = probs.astype(jnp.bfloat16)
            grad_probs = jnp.einsum(
                "qhe,khe->hqk", grad_block, value_heads, preferred_element_type=jnp.float32
            )
            value_grad_acc = value_grad_acc + jnp.einsum(
                "hqk,qhe->khe", probs_low, grad_block, preferred_element_type=jnp.float32
            )
            inner = jnp.sum(grad_probs * probs, axis=2, keepdims=True)
            grad_scores = (probs * (grad_probs - inner)).astype(jnp.bfloat16)
            query_grad = (
                jnp.einsum(
                    "hqk,khe->qhe", grad_scores, key_heads, preferred_element_type=jnp.float32
                )
                * factor
            )
            key_grad_acc = (
                key_grad_acc
                + jnp.einsum(
                    "hqk,qhe->khe", grad_scores, query_block, preferred_element_type=jnp.float32
                )
                * factor
            )
            return ((key_grad_acc, value_grad_acc), query_grad.reshape(block_rows, width))

        empty = jnp.zeros((length, HEADS, HEAD_DIM), jnp.float32)
        (key_grad, value_grad), query_grads = lax.scan(
            one_block, (empty, empty), jnp.arange(blocks)
        )
        return (
            query_grads.reshape(length, width),
            key_grad.reshape(length, width),
            value_grad.reshape(length, width),
        )

    return lax.map(one_sequence, (query, key_rows, value_rows, seg_rows, log_totals, grad_context))


def attention_forward(hidden, seg_rows, first_full, vector_full):
    width = hidden.shape[1]
    seq_count, length = seg_rows.shape
    rounded = hidden.astype(jnp.bfloat16)
    projected = jnp.dot(rounded, first_full[:, : 3 * width], preferred_element_type=jnp.float32)
    query = (projected[:, :width] + vector_full[0]).astype(jnp.bfloat16)
    key_rows = projected[:, width : 2 * width].astype(jnp.bfloat16)
    value_rows = (projected[:, 2 * width :] + vector_full[1]).astype(jnp.bfloat16)
    contexts, log_totals = attention_core(
        query.reshape(seq_count, length, width),
        key_rows.reshape(seq_count, length, width),
        value_rows.reshape(seq_count, length, width),
        seg_rows,
    )
    context_low = contexts.reshape(seq_count * length, width).astype(jnp.bfloat16)
    branch = (
        jnp.dot(context_low, first_full[:, 3 * width :], preferred_element_type=jnp.float32)
        + vector_full[4]
    )
    resid = hidden + branch
    output_rows = layer_norm(resid, vector_full[5], vector_full[6]).astype(jnp.bfloat16)
    wide = jnp.concatenate([query, key_rows, value_rows, context_low], axis=1).astype(jnp.float32)
    return (output_rows, rounded, resid, wide, log_totals)


def feed_forward(hidden, first_full, second_full, vector_full, totals_shape):
    width = hidden.shape[1]
    rounded = hidden.astype(jnp.bfloat16)
    upper = jnp.dot(rounded, first_full, preferred_element_type=jnp.float32) + vector_full[
        0:4
    ].reshape(4 * width)
    active = jax.nn.gelu(upper, approximate=False).astype(jnp.bfloat16)
    branch = jnp.dot(active, second_full, preferred_element_type=jnp.float32) + vector_full[4]
    resid = hidden + branch
    output_rows = layer_norm(resid, vector_full[5], vector_full[6]).astype(jnp.bfloat16)
    return (output_rows, rounded, resid, upper, jnp.zeros(totals_shape, jnp.float32))


def attention_backward(
    grad_out,
    rounded,
    resid,
    wide,
    log_totals,
    seg_rows,
    scale_rows,
    first_full,
    vector_full,
    first_flag,
):
    width = grad_out.shape[1]
    seq_count, length = seg_rows.shape
    grad_resid, gain_grad, shift_grad = norm_backward(grad_out, resid, vector_full[5])
    grad_branch = grad_resid.astype(jnp.bfloat16)
    query = wide[:, :width].astype(jnp.bfloat16)
    key_rows = wide[:, width : 2 * width].astype(jnp.bfloat16)
    value_rows = wide[:, 2 * width : 3 * width].astype(jnp.bfloat16)
    context_low = wide[:, 3 * width :].astype(jnp.bfloat16)
    out_weight_grad = contract_rows(context_low, grad_branch)
    grad_context = contract_cols(grad_branch, first_full[:, 3 * width :]).astype(jnp.bfloat16)
    query_grad, key_grad, value_grad = attention_core_back(
        query.reshape(seq_count, length, width),
        key_rows.reshape(seq_count, length, width),
        value_rows.reshape(seq_count, length, width),
        seg_rows,
        log_totals,
        grad_context.reshape(seq_count, length, width),
    )
    grad_proj = jnp.concatenate(
        [
            query_grad.reshape(-1, width).astype(jnp.bfloat16),
            key_grad.reshape(-1, width).astype(jnp.bfloat16),
            value_grad.reshape(-1, width).astype(jnp.bfloat16),
        ],
        axis=1,
    )
    proj_weight_grad = contract_rows(rounded, grad_proj)
    grad_first = jnp.concatenate([proj_weight_grad, out_weight_grad], axis=1)
    grad_hidden = grad_resid + contract_cols(grad_proj, first_full[:, : 3 * width])
    per_sequence = jnp.sum(grad_hidden.reshape(seq_count, length, width), axis=1)
    time_flag = first_flag.astype(jnp.float32)
    time_weight_grad = jnp.sum(scale_rows[:, None] * per_sequence, axis=0) * time_flag
    time_shift_grad = jnp.sum(per_sequence, axis=0) * time_flag
    proj_sums = jnp.sum(grad_proj.astype(jnp.float32), axis=0)
    grad_vec = jnp.stack(
        [
            proj_sums[:width],
            proj_sums[2 * width :],
            time_weight_grad,
            time_shift_grad,
            jnp.sum(grad_branch.astype(jnp.float32), axis=0),
            gain_grad,
            shift_grad,
        ]
    )
    return (grad_hidden, grad_first, jnp.zeros((FF, width), jnp.float32), grad_vec)


def feed_backward(grad_out, rounded, resid, upper, first_full, second_full, vector_full):
    width = grad_out.shape[1]
    grad_resid, gain_grad, shift_grad = norm_backward(grad_out, resid, vector_full[5])
    grad_branch = grad_resid.astype(jnp.bfloat16)
    active = jax.nn.gelu(upper, approximate=False).astype(jnp.bfloat16)
    grad_second = contract_rows(active, grad_branch)
    grad_active = contract_cols(grad_branch, second_full)
    grad_upper = (grad_active * gelu_slope(upper)).astype(jnp.bfloat16)
    grad_first = contract_rows(rounded, grad_upper)
    grad_hidden = grad_resid + contract_cols(grad_upper, first_full)
    upper_sums = jnp.sum(grad_upper.astype(jnp.float32), axis=0).reshape(4, width)
    tail_rows = jnp.stack([jnp.sum(grad_branch.astype(jnp.float32), axis=0), gain_grad, shift_grad])
    return (grad_hidden, grad_first, grad_second, jnp.concatenate([upper_sums, tail_rows], axis=0))


def store_slot(buffer, value, slot, flag):
    previous = lax.dynamic_index_in_dim(buffer, slot, 0, keepdims=False)
    return lax.dynamic_update_index_in_dim(buffer, jnp.where(flag, value, previous), slot, 0)


def add_totals(backward_fn):

    def run(totals, *rest):
        grad_hidden, grad_first, grad_second, grad_vec = backward_fn(*rest)
        return (
            grad_hidden,
            (totals[0] + grad_first, totals[1] + grad_second, totals[2] + grad_vec),
        )

    return run


def local(inputs, segments, timestep, weight_in, weight_out, vectors, cotangent):
    sections = lax.axis_size("section")
    section_id = lax.axis_index("section")
    first_flag = section_id == 0
    last_flag = section_id == sections - 1
    feed_flag = section_id % 2
    local_seqs, length, width = inputs.shape
    token_rows = MB_SEQS * length
    block_rows = min(512, length)
    totals_shape = (MB_SEQS, length // block_rows, HEADS, block_rows)
    first_full, vector_low = (
        lax.all_gather(weight_in[0], "batch", axis=0, tiled=True),
        lax.all_gather(vectors[0], "batch", axis=1, tiled=True),
    )
    vector_full = vector_low.astype(jnp.float32)
    second_full = lax.all_gather(weight_out[0], "batch", axis=0, tiled=True)
    micro_segments = segments.reshape(MICRO, MB_SEQS, length)
    micro_scale = (timestep.astype(jnp.float32) / STEPS).reshape(MICRO, MB_SEQS)

    def skip_forward(hidden, seg_rows):
        return (
            jnp.zeros((token_rows, width), jnp.bfloat16),
            jnp.zeros((token_rows, width), jnp.bfloat16),
            jnp.zeros((token_rows, width), jnp.float32),
            jnp.zeros((token_rows, FF), jnp.float32),
            jnp.zeros(totals_shape, jnp.float32),
        )

    def attend_branch(hidden, seg_rows):
        return attention_forward(hidden, seg_rows, first_full, vector_full)

    def feed_branch(hidden, seg_rows):
        return feed_forward(hidden, first_full, second_full, vector_full, totals_shape)

    ticks = MICRO + sections - 1
    saved_rounded = jnp.zeros((MICRO, token_rows, width), jnp.bfloat16)
    saved_resid = jnp.zeros((MICRO, token_rows, width), jnp.float32)
    saved_wide = jnp.zeros((MICRO, token_rows, FF), jnp.float32)
    saved_totals = jnp.zeros((MICRO,) + totals_shape, jnp.float32)
    final_rows = jnp.zeros((MICRO, token_rows, width), jnp.bfloat16)
    arriving = jnp.zeros((token_rows, width), jnp.bfloat16)
    for tick_index in range(ticks):
        micro_index = tick_index - section_id
        active_flag = (micro_index >= 0) & (micro_index < MICRO)
        slot = jnp.clip(micro_index, 0, MICRO - 1)
        own_rows = lax.dynamic_index_in_dim(inputs, slot, 0, keepdims=False).astype(jnp.float32)
        seg_rows = lax.dynamic_index_in_dim(micro_segments, slot, 0, keepdims=False)
        scale_rows = lax.dynamic_index_in_dim(micro_scale, slot, 0, keepdims=False)
        embedding = scale_rows[:, None, None] * vector_full[2] + vector_full[3]
        embedding = jnp.broadcast_to(embedding, (MB_SEQS, length, width)).reshape(token_rows, width)
        hidden = jnp.where(first_flag, own_rows + embedding, arriving.astype(jnp.float32))
        branch_index = jnp.where(active_flag, 1 + feed_flag, 0)
        output_rows, rounded, resid, wide, log_totals = lax.switch(
            branch_index, [skip_forward, attend_branch, feed_branch], hidden, seg_rows
        )
        saved_rounded = store_slot(saved_rounded, rounded, slot, active_flag)
        saved_resid = store_slot(saved_resid, resid, slot, active_flag)
        saved_wide = store_slot(saved_wide, wide, slot, active_flag)
        saved_totals = store_slot(saved_totals, log_totals, slot, active_flag)
        final_rows = store_slot(final_rows, output_rows, slot, active_flag & last_flag)
        if tick_index < ticks - 1:
            arriving = jax.tree.map(
                lambda part, own: part.astype(own.dtype),
                shifted(as_sent(output_rows), "section", 1),
                output_rows,
            )

    def skip_keep(totals, grad_out, rounded, resid, wide, log_totals, seg_rows, scale_rows):
        return (jnp.zeros((token_rows, width), jnp.float32), totals)

    def attend_back_branch(grad_out, rounded, resid, wide, log_totals, seg_rows, scale_rows):
        return attention_backward(
            grad_out,
            rounded,
            resid,
            wide,
            log_totals,
            seg_rows,
            scale_rows,
            first_full,
            vector_full,
            first_flag,
        )

    def feed_back_branch(grad_out, rounded, resid, wide, log_totals, seg_rows, scale_rows):
        return feed_backward(grad_out, rounded, resid, wide, first_full, second_full, vector_full)

    totals_now = (
        jnp.zeros((width, FF), jnp.float32),
        jnp.zeros((FF, width), jnp.float32),
        jnp.zeros((7, width), jnp.float32),
    )
    input_grads = jnp.zeros((MICRO, token_rows, width), jnp.float32)
    arriving_grad = jnp.zeros((token_rows, width), jnp.bfloat16)
    for tick_index in range(ticks):
        micro_index = tick_index - (sections - 1 - section_id)
        active_flag = (micro_index >= 0) & (micro_index < MICRO)
        slot = jnp.clip(micro_index, 0, MICRO - 1)
        own_grad = lax.dynamic_index_in_dim(cotangent, slot, 0, keepdims=False).astype(jnp.float32)
        grad_out = jnp.where(last_flag, own_grad, arriving_grad.astype(jnp.float32))
        branch_index = jnp.where(active_flag, 1 + feed_flag, 0)
        loaded = (
            grad_out,
            lax.dynamic_index_in_dim(saved_rounded, slot, 0, keepdims=False),
            lax.dynamic_index_in_dim(saved_resid, slot, 0, keepdims=False),
            lax.dynamic_index_in_dim(saved_wide, slot, 0, keepdims=False),
            lax.dynamic_index_in_dim(saved_totals, slot, 0, keepdims=False),
            lax.dynamic_index_in_dim(micro_segments, slot, 0, keepdims=False),
            lax.dynamic_index_in_dim(micro_scale, slot, 0, keepdims=False),
        )
        grad_hidden, totals_now = lax.switch(
            branch_index,
            [skip_keep, add_totals(attend_back_branch), add_totals(feed_back_branch)],
            totals_now,
            *loaded
        )
        input_grads = store_slot(input_grads, grad_hidden, slot, active_flag & first_flag)
        if tick_index < ticks - 1:
            arriving_grad = shifted(grad_hidden.astype(jnp.bfloat16), "section", -1)
    first_shard, second_shard, vector_shard = (
        lax.psum_scatter(totals_now[0], "batch", scatter_dimension=0, tiled=True),
        lax.psum_scatter(totals_now[1], "batch", scatter_dimension=0, tiled=True),
        lax.psum_scatter(totals_now[2], "batch", scatter_dimension=1, tiled=True),
    )
    result_term = jnp.where(last_flag, final_rows.astype(jnp.float32), 0.0)
    input_term = jnp.where(first_flag, input_grads, 0.0)
    output_part, input_part = (
        lax.psum_scatter(
            result_term.astype(jnp.bfloat16), "section", scatter_dimension=1, tiled=True
        ).astype(jnp.float32),
        lax.psum_scatter(
            input_term.astype(jnp.bfloat16), "section", scatter_dimension=1, tiled=True
        ).astype(jnp.float32),
    )
    output_low = output_part.astype(jnp.bfloat16)
    return (output_low, input_part, first_shard[None], second_shard[None], vector_shard[None])


def solution(mesh):
    return jax.shard_map(
        local,
        mesh=mesh,
        in_specs=(
            P("batch", None, None),
            P("batch", None),
            P("batch"),
            P("section", "batch", None),
            P("section", "batch", None),
            P("section", None, "batch"),
            P("batch", None, None),
        ),
        out_specs=(
            P("batch", "section", None),
            P("batch", "section", None),
            P("section", "batch", None),
            P("section", "batch", None),
            P("section", None, "batch"),
        ),
        check_vma=False,
    )
```

profile of v0, /device:TPU:0, one launch (start us, length us, event | category | flops | bytes accessed | tf_op | source)
XLA Modules:
  0.0 1442.1 jit_solution(15058007280842506202)
XLA Ops:
  10.6 28.3 %all-gather = bf16[1,7,1024]{2,1,0:T(8,128)(2,1)S(1)} all-gather(bf16[1,7,128]{2,1,0:T(8,128)(2,1)} %param.42), channel_id=2, replica_groups=mesh['section'=4,'batch'=8] {'batch'}, dimensions={2}, use_global_device_ids=true | all-gather | bytes 16128 | tf_op jit(solution)/shard_map/all_gather | solution.py:322
  41.1 3.7 multiply_add_fusion
  45.0 93.1 %all-gather.6.cloned.1.call-done = bf16[1,1024,4096]{2,1,0:T(8,128)(2,1)} async-done(((bf16[1,128,4096]{2,1,0:T(8,128)(2,1)}), bf16[1,1024,4096]{2,1,0:T(8,128)(2,1)}) %all-gather.6.cloned.1.call-update) | async-done | bytes 8388624 | tf_op jit(solution)/shard_map/all_gather | solution.py:321
  138.2 125.3 %all-gather.8.cloned.1.call-done = bf16[1,4096,1024]{2,1,0:T(8,128)(2,1)} async-done(((bf16[1,512,1024]{2,1,0:T(8,128)(2,1)}), bf16[1,4096,1024]{2,1,0:T(8,128)(2,1)}) %all-gather.8.cloned.1.call-update) | async-done | bytes 8388624 | tf_op jit(solution)/shard_map/all_gather | solution.py:325
  263.4 33.4 %conditional.10 = (bf16[256,1024]{1,0:T(8,128)(2,1)}, bf16[256,1024]{1,0:T(8,128)(2,1)}, f32[256,1024]{1,0:T(8,128)}, f32[256,4096]{1,0:T(8,128)}, f32[1,1,16,256]{3,2,1,0:T(8,128)S(1)}) conditional(s32[]{:T(128)} %clamp.30, () %tuple.208, (f32[256,1024]{1,0:T(8,128)S(1)}, bf16[1024,4096]{1,0:T(8,128)(2,1)}, ...), branch_computations={%region_0.1_spmd, %region_1.6_spmd, %region_6.9_spmd} | conditional | flops 4367319552 | bytes 65478784 | solution.py:362
  264.3 4.8 fusion
  278.7 3.5 fusion.1024
  303.9 2.9 bitcast_dynamic-update-slice_fusion.4
  309.2 3.5 copy-done
  313.2 41.6 %conditional.11 = (bf16[256,1024]{1,0:T(8,128)(2,1)}, bf16[256,1024]{1,0:T(8,128)(2,1)}, f32[256,1024]{1,0:T(8,128)}, f32[256,4096]{1,0:T(8,128)}, f32[1,1,16,256]{3,2,1,0:T(8,128)S(1)}) conditional(s32[]{:T(128)} %clamp.31, () %tuple.211, (f32[256,1024]{1,0:T(8,128)S(1)}, bf16[1024,4096]{1,0:T(8,128)(2,1)S(1)}, ...), branch_computations={%region_9.10_spmd, %region_10.15_spmd, %region_15.18_spmd} | conditional | flops 4367319552 | bytes 107421904 | solution.py:362
  315.5 3.2 fusion.96
  334.4 3.5 fusion.1028
  343.7 4.0 maximum_convert_fusion.1
  361.2 5.3 bitcast_dynamic-update-slice_fusion.3
  366.6 4.8 constant_dynamic-slice_fusion.24
  371.6 12.0 conditional.12
  389.4 2.7 bitcast_dynamic-update-slice_fusion.2
  392.1 5.3 constant_dynamic-slice_fusion.23
  397.6 12.2 conditional.13
  409.9 5.6 collective-permute-start.3
  421.8 5.3 constant_dynamic-slice_fusion.22
  427.3 10.6 conditional.14
  440.6 4.8 bitcast_dynamic-update-slice_fusion
  445.4 4.7 dynamic-slice_bitcast_fusion.10
  451.5 7.1 dynamic-slice_bitcast_fusion.5
  460.4 26.4 %conditional.15 = (f32[256,1024]{1,0:T(8,128)}, f32[1024,4096]{0,1:T(8,128)}, f32[4096,1024]{1,0:T(8,128)}, f32[7,1024]{1,0:T(8,128)S(1)}) conditional(s32[]{:T(128)} %clamp.35, () %tuple.223, (f32[256,1024]{1,0:T(8,128)S(1)}, f32[7,1024]{1,0:T(8,128)S(1)}, f32[256,1024]{1,0:T(8,128)}, s32[2,256]{1,0:T(2,128)S(1)}, s32[]{:T(128)}, ...), branch_computations={%region_46.47_spmd, %region_47.58_spmd, %region_58.67_spmd} | conditional | flops 8677505024 | bytes 180885728 | solution.py:420
  461.5 7.9 broadcast_in_dim.600
  469.4 7.8 broadcast_in_dim.601
  489.3 26.0 %collective-permute-done.4 = bf16[256,1024]{1,0:T(8,128)(2,1)S(1)} collective-permute-done((bf16[256,1024]{1,0:T(8,128)(2,1)S(1)}, bf16[256,1024]{1,0:T(8,128)(2,1)S(1)}, u32[]{:S(2)}, u32[]{:S(2)}) %collective-permute-start.4) | collective-permute-done | bytes 524320 | tf_op jit(solution)/shard_map/ppermute | solution.py:27
  516.6 3.1 conditional.16
  523.5 9.9 collective-permute-done.5
  535.7 3.9 conditional.17
  544.0 102.1 %collective-permute-done.6 = bf16[256,1024]{1,0:T(8,128)(2,1)S(1)} collective-permute-done((bf16[256,1024]{1,0:T(8,128)(2,1)S(1)}, bf16[256,1024]{1,0:T(8,128)(2,1)S(1)}, u32[]{:S(2)}, u32[]{:S(2)}) %collective-permute-start.6) | collective-permute-done | bytes 524320 | tf_op jit(solution)/shard_map/ppermute | solution.py:27
  647.3 43.5 %conditional.18 = (f32[256,1024]{1,0:T(8,128)}, f32[1024,4096]{0,1:T(8,128)}, f32[4096,1024]{1,0:T(8,128)}, f32[7,1024]{1,0:T(8,128)S(1)}) conditional(s32[]{:T(128)} %clamp.38, (f32[1024,4096]{0,1:T(8,128)}, f32[4096,1024]{1,0:T(8,128)}, f32[7,1024]{1,0:T(8,128)S(1)}) %tuple.232, (f32[256,1024]{1,0:T(8,128)S(1)}, ...), branch_computations={%region_109.110_spmd, %region_110.121_spmd, %region_121.130_spmd} | conditional | flops 8685900800 | bytes 176777408 | solution.py:420
  654.6 4.9 copy.116
  666.8 2.9 fusion.1054
  673.4 12.5 maximum_add_fusion.4
  696.2 16.2 %collective-permute-done.7 = bf16[256,1024]{1,0:T(8,128)(2,1)S(1)} collective-permute-done((bf16[256,1024]{1,0:T(8,128)(2,1)S(1)}, bf16[256,1024]{1,0:T(8,128)(2,1)S(1)}, u32[]{:S(2)}, u32[]{:S(2)}) %collective-permute-start.7) | collective-permute-done | bytes 524320 | tf_op jit(solution)/shard_map/ppermute | solution.py:27
  713.5 43.2 %conditional.19 = (f32[256,1024]{1,0:T(8,128)}, f32[1024,4096]{0,1:T(8,128)}, f32[4096,1024]{1,0:T(8,128)}, f32[7,1024]{1,0:T(8,128)S(1)}) conditional(s32[]{:T(128)} %clamp.39, (f32[1024,4096]{0,1:T(8,128)}, f32[4096,1024]{1,0:T(8,128)}, f32[7,1024]{1,0:T(8,128)S(1)}) %tuple.235, (f32[256,1024]{1,0:T(8,128)S(1)}, ...), branch_computations={%region_130.131_spmd, %region_131.142_spmd, %region_142.151_spmd} | conditional | flops 8685900800 | bytes 176777408 | solution.py:420
  720.8 4.9 copy.117
  732.9 2.9 fusion.1057
  739.5 12.5 maximum_add_fusion.6
  763.0 17.5 %copy.118 = f32[1024,4096]{1,0:T(8,128)} copy(f32[1024,4096]{0,1:T(8,128)} %get-tuple-element.1593) | data formatting | bytes 33554432 | tf_op jit(solution)/shard_map/cond | solution.py:420
  781.3 26.9 %reduce-scatter.14.cloned.1.call-done = f32[7,128]{1,0:T(8,128)} async-done(((f32[7,1024]{1,0:T(8,128)}), f32[7,128]{1,0:T(8,128)}) %reduce-scatter.14.cloned.1.call-update) | async-done | bytes 3600 | tf_op jit(solution)/shard_map/reduce_scatter | solution.py:432
  809.5 25.1 %reduce-scatter.8.cloned.1.call-done = bf16[2,64,1024]{2,1,0:T(8,128)(2,1)} async-done(((bf16[2,256,1024]{2,1,0:T(8,128)(2,1)}), bf16[2,64,1024]{2,1,0:T(8,128)(2,1)}) %reduce-scatter.8.cloned.1.call-update) | async-done | bytes 262160 | tf_op jit(solution)/shard_map/reduce_scatter | solution.py:440
  836.4 26.2 %reduce-scatter.6.cloned.1.call-done = bf16[2,64,1024]{2,1,0:T(8,128)(2,1)} async-done(((bf16[2,256,1024]{2,1,0:T(8,128)(2,1)}), bf16[2,64,1024]{2,1,0:T(8,128)(2,1)}) %reduce-scatter.6.cloned.1.call-update) | async-done | bytes 262160 | tf_op jit(solution)/shard_map/reduce_scatter | solution.py:437
  862.6 286.1 %reduce-scatter.10.cloned.1.call-done = f32[128,4096]{1,0:T(8,128)} async-done(((f32[1024,4096]{1,0:T(8,128)}), f32[128,4096]{1,0:T(8,128)}) %reduce-scatter.10.cloned.1.call-update) | async-done | bytes 2097168 | tf_op jit(solution)/shard_map/reduce_scatter | solution.py:430
  1148.7 286.2 %reduce-scatter.12.cloned.1.call-done = f32[512,1024]{1,0:T(8,128)} async-done(((f32[4096,1024]{1,0:T(8,128)}), f32[512,1024]{1,0:T(8,128)}) %reduce-scatter.12.cloned.1.call-update) | async-done | bytes 2097168 | tf_op jit(solution)/shard_map/reduce_scatter | solution.py:431
  (321 shorter events, 171.6 us)
Async XLA Ops:
  7.2 37.7 %copy-start.37 = (bf16[2,256,1024]{2,1,0:T(8,128)(2,1)S(1)}, bf16[2,256,1024]{2,1,0:T(8,128)(2,1)}, u32[]{:S(2)}) copy-start(bf16[2,256,1024]{2,1,0:T(8,128)(2,1)} %param.37) | copy-start | bytes 3145732
  7.2 256.2 %copy-start.90 = (s32[2,256]{1,0:T(2,128)S(1)}, s32[2,256]{1,0:T(2,128)}, u32[]{:S(2)}) copy-start(s32[2,256]{1,0:T(2,128)} %param.38) | copy-start | bytes 6148
  7.2 131.0 %all-gather.6.cloned.1.call-start = ((), (), s32[]{:S(2)}) async-start(), calls=%async_computation.10 | async-start | bytes 9437184 | tf_op jit(solution)/shard_map/all_gather | solution.py:321
  7.9 255.5 %all-gather.8.cloned.1.call-start = ((), (), s32[]{:S(2)}) async-start(), calls=%async_computation.11 | async-start | bytes 9437184 | tf_op jit(solution)/shard_map/all_gather | solution.py:325
  8.7 799.6 %reduce-scatter.14.cloned.1.call-start = ((), (), s32[]{:S(2)}) async-start(), calls=%async_computation.9 | async-start | bytes 36864 | tf_op jit(solution)/shard_map/reduce_scatter | solution.py:432
  278.7 5.0 copy-start.74
  296.9 15.9 %collective-permute-start = (bf16[256,1024]{1,0:T(8,128)(2,1)}, bf16[256,1024]{1,0:T(8,128)(2,1)S(1)}, u32[]{:S(2)}, u32[]{:S(2)}) collective-permute-start(bf16[256,1024]{1,0:T(8,128)(2,1)} %get-tuple-element.1551), channel_id=1, source_target_pairs={{0,8},{8,16},{16,24},{1,9},{9,17},{17,25},{2,10},{10,18},{18,26},{... | collective-permute-start | bytes 1572872 | tf_op jit(solution)/shard_map/ppermute | solution.py:27
  303.9 9.0 slice-start
  306.8 5.9 copy-start
  306.9 5.9 copy-start.38
  306.9 6.3 slice-start.1
  313.2 5.6 copy-start.32
  354.8 4.4 copy-start.71
  354.8 6.4 copy-start.8
  354.8 16.5 %collective-permute-start.1 = (bf16[256,1024]{1,0:T(8,128)(2,1)}, bf16[256,1024]{1,0:T(8,128)(2,1)S(1)}, u32[]{:S(2)}, u32[]{:S(2)}) collective-permute-start(bf16[256,1024]{1,0:T(8,128)(2,1)} %get-tuple-element.1552), channel_id=1, source_target_pairs={{0,8},{8,16},{16,24},{1,9},{9,17},{17,25},{2,10},{10,18},{18,26},{... | collective-permute-start | bytes 1572872 | tf_op jit(solution)/shard_map/ppermute | solution.py:27
  360.4 11.1 slice-start.2
  361.2 10.3 slice-start.3
  366.6 4.8 copy-start.39
  383.5 4.8 copy-start.72
  383.6 5.8 copy-start.9
  383.6 13.8 collective-permute-start.2
  388.6 9.1 slice-start.4
  389.4 8.2 slice-start.5
  392.1 5.3 copy-start.40
  392.1 5.3 copy-start.92
  409.9 8.1 copy-start.73
  409.9 9.1 copy-start.10
  409.9 17.1 %collective-permute-start.3 = (bf16[256,1024]{1,0:T(8,128)(2,1)}, bf16[256,1024]{1,0:T(8,128)(2,1)S(1)}, u32[]{:S(2)}, u32[]{:S(2)}) collective-permute-start(bf16[256,1024]{1,0:T(8,128)(2,1)} %get-tuple-element.1554), channel_id=1, source_target_pairs={{0,8},{8,16},{16,24},{1,9},{9,17},{17,25},{2,10},{10,18},{18,26},{... | collective-permute-start | bytes 1572872 | tf_op jit(solution)/shard_map/ppermute | solution.py:27
  418.2 9.1 slice-start.6
  419.0 8.2 slice-start.7
  421.8 5.3 copy-start.41
  421.8 5.3 copy-start.91
  445.4 6.1 copy-start.1
  451.5 7.1 copy-start.70
  488.0 27.3 %collective-permute-start.4 = (bf16[256,1024]{1,0:T(8,128)(2,1)S(1)}, bf16[256,1024]{1,0:T(8,128)(2,1)S(1)}, u32[]{:S(2)}, u32[]{:S(2)}) collective-permute-start(bf16[256,1024]{1,0:T(8,128)(2,1)S(1)} %convert_element_type.868), channel_id=1, source_target_pairs={{8,0},{16,8},{24,16},{9,1},{17,9},{25,17},{10,2},{18,10},{26,18},{... | collective-permute-start | bytes 1572872 | tf_op jit(solution)/shard_map/ppermute | solution.py:27
  520.7 12.7 collective-permute-start.5
  522.0 13.7 copy-start.4
  540.9 105.2 %copy-start.42 = (bf16[2,256,1024]{2,1,0:T(8,128)(2,1)S(1)}, bf16[2,256,1024]{2,1,0:T(8,128)(2,1)}, u32[]{:S(2)}) copy-start(bf16[2,256,1024]{2,1,0:T(8,128)(2,1)} %param.43) | copy-start | bytes 3145732
  540.9 105.2 %collective-permute-start.6 = (bf16[256,1024]{1,0:T(8,128)(2,1)S(1)}, bf16[256,1024]{1,0:T(8,128)(2,1)S(1)}, u32[]{:S(2)}, u32[]{:S(2)}) collective-permute-start(bf16[256,1024]{1,0:T(8,128)(2,1)S(1)} %convert_element_type.876), channel_id=1, source_target_pairs={{8,0},{16,8},{24,16},{9,1},{17,9},{25,17},{10,2},{18,10},{26,18},{... | collective-permute-start | bytes 1572872 | tf_op jit(solution)/shard_map/ppermute | solution.py:27
  543.7 103.6 %copy-start.3 = (f32[256,1024]{1,0:T(8,128)S(1)}, f32[256,1024]{1,0:T(8,128)}, u32[]{:S(2)}) copy-start(f32[256,1024]{1,0:T(8,128)} %get-tuple-element.1961) | copy-start | bytes 3145732
  690.8 21.5 %copy-start.43 = (bf16[2,256,1024]{2,1,0:T(8,128)(2,1)S(1)}, bf16[2,256,1024]{2,1,0:T(8,128)(2,1)}, u32[]{:S(2)}) copy-start(bf16[2,256,1024]{2,1,0:T(8,128)(2,1)} %param.43) | copy-start | bytes 3145732
  692.2 20.1 %collective-permute-start.7 = (bf16[256,1024]{1,0:T(8,128)(2,1)S(1)}, bf16[256,1024]{1,0:T(8,128)(2,1)S(1)}, u32[]{:S(2)}, u32[]{:S(2)}) collective-permute-start(bf16[256,1024]{1,0:T(8,128)(2,1)S(1)} %convert_element_type.880), channel_id=1, source_target_pairs={{8,0},{16,8},{24,16},{9,1},{17,9},{25,17},{10,2},{18,10},{26,18},{... | collective-permute-start | bytes 1572872 | tf_op jit(solution)/shard_map/ppermute | solution.py:27
  693.7 19.8 %copy-start.2 = (f32[256,1024]{1,0:T(8,128)S(1)}, f32[256,1024]{1,0:T(8,128)}, u32[]{:S(2)}) copy-start(f32[256,1024]{1,0:T(8,128)} %get-tuple-element.1960) | copy-start | bytes 3145732
  728.9 3.8 slice-start.24
  757.3 77.2 %reduce-scatter.8.cloned.1.call-start = ((), (), s32[]{:S(2)}) async-start(), calls=%async_computation.6 | async-start | bytes 1310720 | tf_op jit(solution)/shard_map/reduce_scatter | solution.py:440
  760.3 102.3 %reduce-scatter.6.cloned.1.call-start = ((), (), s32[]{:S(2)}) async-start(), calls=%async_computation.5 | async-start | bytes 1310720 | tf_op jit(solution)/shard_map/reduce_scatter | solution.py:437
  763.0 385.8 %reduce-scatter.10.cloned.1.call-start = ((), (), s32[]{:S(2)}) async-start(), calls=%async_computation.7 | async-start | bytes 18874368 | tf_op jit(solution)/shard_map/reduce_scatter | solution.py:430
  780.5 654.4 %reduce-scatter.12.cloned.1.call-start = ((), (), s32[]{:S(2)}) async-start(), calls=%async_computation.8 | async-start | bytes 18874368 | tf_op jit(solution)/shard_map/reduce_scatter | solution.py:431
  (21 other events, 38.7 us)
Sparse Core Ops, SparseCore 0:
  10.1 127.9 all-gather.5
  140.3 123.0 all-gather.7
  757.4 50.7 reduce-scatter.13
  810.6 23.9 reduce-scatter.7
  837.7 24.8 reduce-scatter.5
  866.8 281.8 reduce-scatter.9
  1153.6 281.3 reduce-scatter.11
where the time goes:
time: 1450 us; the launch traced here: 1440 us
  waiting for transfers between devices  1030 us (71%)
  local copies, waits for them, and re-layouts  140 us (10%)
  other arithmetic  114 us (8%)
  loops' own time  55.1 us (4%)
  matrix products  47.7 us (3%)
  blocking collectives  28.3 us (2%)
  starting transfers between devices  16.5 us (1%)
  between operations  15.4 us (1%)
    reduce_scatter x1, waiting for transfers between devices, local(): lax.psum_scatter(totals_now[1], 'batch', scatter_dimension=0, tiled=True)  286 us
    reduce_scatter x1, waiting for transfers between devices, local(): lax.psum_scatter(totals_now[0], 'batch', scatter_dimension=0, tiled=True)  286 us
    ppermute x8, waiting for transfers between devices, shifted(): return lax.ppermute(block, axis, route)  154 us
    all_gather x1, waiting for transfers between devices, local(): second_full = lax.all_gather(weight_out[0], 'batch', axis=0, tiled=True)  125 us
    all_gather x1, waiting for transfers between devices, local(): lax.all_gather(weight_in[0], 'batch', axis=0, tiled=True)  93.1 us
    dynamic_update_slice x30, other arithmetic, store_slot(): lax.dynamic_update_index_in_dim(buffer, jnp.where(flag, value, previous),...  34.3 us
    another operation x5, loops' own time, local(): lax.switch(branch_index, [skip_forward, attend_branch, feed_branch], hidd...  33.4 us
  transfers between devices with their start and end apart: 15, of which 11 were waited for; matrix products, arithmetic and copies ran while one was open for 6% of the time, Pallas kernels for 0%

commit v1 on v0

v1 whole, which is shorter than its diff:
```python
import functools
import math

import jax
import jax.numpy as jnp
from jax import lax
from jax.experimental import pallas as pl
from jax.experimental.pallas import tpu as pltpu
from jax.sharding import PartitionSpec as P

STEPS = 5000
SECTIONS = 4
BLOCKS = 8
LANES = 128
HEAD_DIM = 64

norm_eps = 1e-05
masked_score = -1e30
f32, bf16 = jnp.float32, jnp.bfloat16

VMEM = pl.BlockSpec(memory_space=pltpu.VMEM)
SMEM = pl.BlockSpec(memory_space=pltpu.SMEM)
ANY = pl.BlockSpec(memory_space=pl.ANY)


def dot_nn(a, b):
    return jnp.dot(a, b, preferred_element_type=f32)


def dot_nt(a, b):
    return lax.dot_general(a, b, (((1,), (1,)), ((), ())), preferred_element_type=f32)


def dot_tn(a, b):
    return lax.dot_general(a, b, (((0,), (0,)), ((), ())), preferred_element_type=f32)


def shape_of(dims, dtype):
    return jax.ShapeDtypeStruct(dims, dtype)


def kernel_call(body, in_specs, outs, args, scratch=(), flops=0, moved=0, limit=40):
    return pl.pallas_call(
        body,
        in_specs=in_specs,
        out_specs=[VMEM] * len(outs),
        out_shape=outs,
        scratch_shapes=list(scratch),
        compiler_params=pltpu.CompilerParams(vmem_limit_bytes=limit * 1024 * 1024),
        cost_estimate=pl.CostEstimate(flops=flops, bytes_accessed=moved, transcendentals=0),
    )(*args)


def block_copies(order, shards, first_row, rows, cols, target, sems, last):
    copies = []
    for j in range(BLOCKS - 1):
        copies.append(
            pltpu.make_async_copy(
                shards[j].at[pl.ds(first_row, rows), pl.ds(0, cols)],
                target.at[pl.ds(pl.multiple_of(order[j] * rows, rows), rows), :],
                sems.at[j],
            )
        )
    base = order[BLOCKS - 1] * rows
    at = BLOCKS - 1
    for piece, (offset, count) in last:
        copies.append(
            pltpu.make_async_copy(
                piece.at[pl.ds(0, count), pl.ds(0, cols)],
                target.at[pl.ds(pl.multiple_of(base + offset, count), count), :],
                sems.at[at],
            )
        )
        at += 1
    return copies


def start_all(copies):
    for copy in copies:
        copy.start()


def wait_all(copies):
    for copy in copies:
        copy.wait()


def attention_copies(order, shards, cols, target, sems):
    half = LANES // 2
    last = [(shards[7], (0, half)), (shards[8], (half, half))]
    return block_copies(order, shards, 0, LANES, cols, target, sems, last)


def feed_copies(order, shards, width, up, down, sems):
    first = block_copies(order, shards, 0, LANES, width, up, sems.at[0], [(shards[7], (0, LANES))])
    second = block_copies(
        order, shards, LANES, LANES, width, down, sems.at[1], [(shards[8], (0, LANES))]
    )
    return first, second


def lane_masks(rows):
    lane = lax.broadcasted_iota(jnp.int32, (rows, LANES), 1)
    return lane < HEAD_DIM, lane >= HEAD_DIM


def seq_rows(ref, seq, cols, half):
    top = ref[seq * LANES : (seq + 1) * LANES, cols]
    bottom = ref[half + seq * LANES : half + (seq + 1) * LANES, cols]
    return jnp.concatenate([top, bottom], axis=0)


def put_rows(ref, seq, cols, half, value):
    ref[seq * LANES : (seq + 1) * LANES, cols] = value[:LANES]
    ref[half + seq * LANES : half + (seq + 1) * LANES, cols] = value[LANES:]


def attend_kernel(order, own, peer, seg, bias, *refs):
    shards, (qkv, probs, ctx, x, w, sems) = refs[:9], refs[9:]
    half, width = own.shape
    seqs = half // LANES
    copies = attention_copies(order, shards, 3 * 256, w, sems)
    start_all(copies)
    x[:half] = own[...]
    x[half:] = peer[...]
    wait_all(copies)
    for i in range(3):
        cols = slice(256 * i, 256 * (i + 1))
        qkv[:, cols] = (dot_nn(x[...], w[:, cols]) + bias[:, cols]).astype(bf16)
    factor = 1.0 / math.sqrt(HEAD_DIM)
    masks = lane_masks(2 * LANES)
    for seq in range(seqs):
        key_seg = jnp.broadcast_to(seg[seq : seq + 1, :], (2 * LANES, 2 * LANES))
        allowed = key_seg == key_seg.T
        for group in range(2):
            q, k, v = [
                seq_rows(qkv, seq, slice(256 * i + LANES * group, 256 * i + LANES * (group + 1)), half)
                for i in range(3)
            ]
            parts = []
            for h in range(2):
                scores = dot_nt(jnp.where(masks[h], q, jnp.zeros_like(q)), k) * factor
                scores = jnp.where(allowed, scores, masked_score)
                peaks = jnp.max(scores, axis=1, keepdims=True)
                exponent = jnp.exp(scores - peaks)
                totals = jnp.sum(exponent, axis=1, keepdims=True)
                weights = exponent * (1.0 / totals)
                probs[(seq * 2 + group) * 2 + h] = weights
                parts.append(dot_nn(weights.astype(bf16), v))
            put_rows(
                ctx,
                seq,
                slice(LANES * group, LANES * (group + 1)),
                half,
                jnp.where(masks[0], parts[0], parts[1]).astype(bf16),
            )


def attend(order, own, peer, seg, bias, shards):
    half, width = own.shape
    seqs = half // LANES
    return kernel_call(
        attend_kernel,
        [SMEM] + [VMEM] * 4 + [ANY] * 9,
        [
            shape_of((2 * half, 768), bf16),
            shape_of((4 * seqs, 2 * LANES, 2 * LANES), f32),
            shape_of((2 * half, 256), bf16),
        ],
        (order, own, peer, seg, bias, *shards),
        [
            pltpu.VMEM((2 * half, width), bf16),
            pltpu.VMEM((width, 768), bf16),
            pltpu.SemaphoreType.DMA((9,)),
        ],
        flops=4 * half * width * 768,
        moved=8 << 20,
    )


def out_blocks(s):
    return slice(LANES * s, LANES * (s + 1)), slice(512 + LANES * s, 512 + LANES * (s + 1))


def project_kernel(ctx, wo, p_own, p_send):
    half = p_own.shape[0]
    for s in range(SECTIONS):
        result = dot_nn(ctx[...], wo[s].reshape(2 * LANES, 2 * LANES))
        for g, cols in enumerate(out_blocks(s)):
            part = result[:, LANES * g : LANES * (g + 1)]
            p_own[:, cols] = part[:half]
            p_send[:, cols] = part[half:].astype(bf16)


def project(ctx, wo, width):
    half = ctx.shape[0] // 2
    return kernel_call(
        project_kernel,
        [VMEM] * 2,
        [shape_of((half, width), f32), shape_of((half, width), bf16)],
        (ctx, wo),
        flops=4 * half * 256 * width,
        moved=3 << 20,
    )


def pack_kernel(order, *refs):
    shards, (packed, sems) = refs[:9], refs[9:]
    copies = []
    for j in range(7):
        b = order[j]
        copies.append(
            pltpu.make_async_copy(
                shards[j].at[:, pl.ds(768, 256)], packed.at[b % SECTIONS, b // SECTIONS], sems.at[j]
            )
        )
    b = order[7]
    half = LANES // 2
    for j in range(2):
        copies.append(
            pltpu.make_async_copy(
                shards[7 + j].at[:, pl.ds(768, 256)],
                packed.at[b % SECTIONS, b // SECTIONS, pl.ds(half * j, half)],
                sems.at[7 + j],
            )
        )
    start_all(copies)
    wait_all(copies)


def pack_out(order, shards):
    (packed,) = kernel_call(
        pack_kernel,
        [SMEM] + [ANY] * 9,
        [shape_of((SECTIONS, 2, LANES, 256), bf16)],
        (order, *shards),
        [pltpu.SemaphoreType.DMA((9,))],
        moved=1 << 20,
    )
    return packed


def out_grad_kernel(own, peer, ctx, packed):
    half = own.shape[0]
    for s in range(SECTIONS):
        cols = jnp.concatenate(
            [
                jnp.concatenate([own[:, c], peer[:, c]], axis=0)
                for c in out_blocks(s)
            ],
            axis=1,
        )
        packed[s] = dot_tn(ctx[...], cols).astype(bf16).reshape(2, LANES, 256)


def out_grad(own, peer, ctx):
    half, width = own.shape
    (packed,) = kernel_call(
        out_grad_kernel,
        [VMEM] * 3,
        [shape_of((SECTIONS, 2, LANES, 256), bf16)],
        (own, peer, ctx),
        flops=4 * half * 256 * width,
        moved=2 << 20,
    )
    return packed


def attend_back_kernel(order, own, peer, wo, qkv, probs, *refs):
    shards, (p_own, p_send, grads, sums, w, gctx, sems) = refs[:9], refs[9:]
    half, width = own.shape
    seqs = half // LANES
    copies = attention_copies(order, shards, 3 * 256, w, sems)
    start_all(copies)
    for part, rows in ((own, slice(0, half)), (peer, slice(half, 2 * half))):
        total = None
        for s in range(SECTIONS):
            cols = jnp.concatenate([part[:, c] for c in out_blocks(s)], axis=1)
            term = dot_nt(cols, wo[s].reshape(2 * LANES, 2 * LANES))
            total = term if total is None else total + term
        gctx[rows, :] = total.astype(bf16)
    factor = 1.0 / math.sqrt(HEAD_DIM)
    masks = lane_masks(2 * LANES)
    for seq in range(seqs):
        for group in range(2):
            lanes = slice(LANES * group, LANES * (group + 1))
            q, k, v = [
                seq_rows(qkv, seq, slice(256 * i + LANES * group, 256 * i + LANES * (group + 1)), half)
                for i in range(3)
            ]
            grad = seq_rows(gctx, seq, lanes, half)
            parts = []
            for h in range(2):
                weights = probs[(seq * 2 + group) * 2 + h]
                grad_probs = dot_nt(jnp.where(masks[h], grad, jnp.zeros_like(grad)), v)
                inner = jnp.sum(grad_probs * weights, axis=1, keepdims=True)
                grad_scores = (weights * (grad_probs - inner)).astype(bf16)
                parts.append(
                    (
                        dot_nn(grad_scores, k) * factor,
                        dot_tn(grad_scores, q) * factor,
                        dot_tn(weights.astype(bf16), grad),
                    )
                )
            for i in range(3):
                value = jnp.where(masks[0], parts[0][i], parts[1][i]).astype(bf16)
                put_rows(
                    grads,
                    seq,
                    slice(256 * i + LANES * group, 256 * i + LANES * (group + 1)),
                    half,
                    value,
                )
    sums[0:1, :] = jnp.sum(grads[...].astype(f32), axis=0, keepdims=True)
    wait_all(copies)
    for i in range(width // 256):
        cols = slice(256 * i, 256 * (i + 1))
        result = dot_nt(grads[...], w[cols, :])
        p_own[:, cols] = result[:half]
        p_send[:, cols] = result[half:].astype(bf16)


def attend_back(order, own, peer, wo, qkv, probs, shards):
    half, width = own.shape
    return kernel_call(
        attend_back_kernel,
        [SMEM] + [VMEM] * 5 + [ANY] * 9,
        [
            shape_of((half, width), f32),
            shape_of((half, width), bf16),
            shape_of((2 * half, 768), bf16),
            shape_of((8, 768), f32),
        ],
        (order, own, peer, wo, qkv, probs, *shards),
        [
            pltpu.VMEM((width, 768), bf16),
            pltpu.VMEM((2 * half, 256), bf16),
            pltpu.SemaphoreType.DMA((9,)),
        ],
        flops=4 * half * width * 1024,
        moved=8 << 20,
    )


def split_outputs(outs, j, row, value):
    if j == 4:
        outs[8 if row else 4][...] = value
    else:
        outs[j][row : row + LANES, :] = value


def pair_cols(parts, first, second):
    return jnp.concatenate(
        [
            jnp.concatenate([part[:, pl.ds(pl.multiple_of(b * LANES, LANES), LANES)] for b in (first, second)], axis=1)
            for part in parts
        ],
        axis=0,
    )


def attend_weight_kernel(slots, own, peer, grads, wo_grad, *outs):
    for j in range(0, BLOCKS, 2):
        first, second = slots[j], slots[j + 1]
        result = dot_tn(pair_cols((own, peer), first, second), grads[...]).astype(bf16)
        for i, b in enumerate((first, second)):
            slot = j + i
            rows = result[LANES * i : LANES * (i + 1)]
            tail = wo_grad[b % SECTIONS, b // SECTIONS]
            if slot == 4:
                mid = LANES // 2
                outs[4][:, :768], outs[4][:, 768:] = rows[:mid], tail[:mid]
                outs[8][:, :768], outs[8][:, 768:] = rows[mid:], tail[mid:]
            else:
                outs[slot][:, :768], outs[slot][:, 768:] = rows, tail


def chunk_shapes(rows, width):
    half = rows // 2
    return [shape_of((half if j in (4, 8) else rows, width), bf16) for j in range(9)]


def attend_weight(slots, own, peer, grads, wo_grad):
    half, width = own.shape
    return kernel_call(
        attend_weight_kernel,
        [SMEM] + [VMEM] * 4,
        chunk_shapes(LANES, width),
        (slots, own, peer, grads, wo_grad),
        flops=4 * half * width * 768,
        moved=5 << 20,
    )


def feed_kernel(order, own, peer, bias, *refs):
    shards, (p_own, p_send, active, slope, x, up, down, sems) = refs[:9], refs[9:]
    half, width = own.shape
    first, second = feed_copies(order, shards, width, up, down, sems)
    start_all(first)
    start_all(second)
    x[:half] = own[...]
    x[half:] = peer[...]
    wait_all(first)
    for i in range(width // 256):
        cols = slice(256 * i, 256 * (i + 1))
        upper = dot_nn(x[...], up[:, cols]) + bias[:, cols]
        cumulative = 0.5 * (1.0 + lax.erf(upper * (1.0 / math.sqrt(2.0))))
        density = jnp.exp(-0.5 * upper * upper) * (1.0 / math.sqrt(2.0 * math.pi))
        active[:, cols] = (upper * cumulative).astype(bf16)
        slope[:, cols] = cumulative + upper * density
    wait_all(second)
    for i in range(width // 256):
        cols = slice(256 * i, 256 * (i + 1))
        result = dot_nn(active[...], down[:, cols])
        p_own[:, cols] = result[:half]
        p_send[:, cols] = result[half:].astype(bf16)


def feed(order, own, peer, bias, shards):
    half, width = own.shape
    return kernel_call(
        feed_kernel,
        [SMEM] + [VMEM] * 3 + [ANY] * 9,
        [
            shape_of((half, width), f32),
            shape_of((half, width), bf16),
            shape_of((2 * half, width), bf16),
            shape_of((2 * half, width), f32),
        ],
        (order, own, peer, bias, *shards),
        [
            pltpu.VMEM((2 * half, width), bf16),
            pltpu.VMEM((width, width), bf16),
            pltpu.VMEM((width, width), bf16),
            pltpu.SemaphoreType.DMA((2, 9)),
        ],
        flops=8 * half * width * width,
        moved=10 << 20,
    )


def feed_back_kernel(order, own, peer, slope, *refs):
    shards, (p_own, p_send, grads, sums, g, up, down, sems) = refs[:9], refs[9:]
    half, width = own.shape
    first, second = feed_copies(order, shards, width, up, down, sems)
    start_all(second)
    start_all(first)
    g[:half] = own[...]
    g[half:] = peer[...]
    wait_all(second)
    for i in range(width // 256):
        cols = slice(256 * i, 256 * (i + 1))
        grad = (dot_nt(g[...], down[cols, :]) * slope[:, cols]).astype(bf16)
        grads[:, cols] = grad
        sums[0:1, cols] = jnp.sum(grad.astype(f32), axis=0, keepdims=True)
    wait_all(first)
    for i in range(width // 256):
        cols = slice(256 * i, 256 * (i + 1))
        result = dot_nt(grads[...], up[cols, :])
        p_own[:, cols] = result[:half]
        p_send[:, cols] = result[half:].astype(bf16)


def feed_back(order, own, peer, slope, shards):
    half, width = own.shape
    return kernel_call(
        feed_back_kernel,
        [SMEM] + [VMEM] * 3 + [ANY] * 9,
        [
            shape_of((half, width), f32),
            shape_of((half, width), bf16),
            shape_of((2 * half, width), bf16),
            shape_of((8, width), f32),
        ],
        (order, own, peer, slope, *shards),
        [
            pltpu.VMEM((2 * half, width), bf16),
            pltpu.VMEM((width, width), bf16),
            pltpu.VMEM((width, width), bf16),
            pltpu.SemaphoreType.DMA((2, 9)),
        ],
        flops=8 * half * width * width,
        moved=10 << 20,
    )


def feed_weight_kernel(slots, own, peer, grads, gown, gpeer, active, *outs):
    g = jnp.concatenate([gown[...], gpeer[...]], axis=0)
    for j in range(0, BLOCKS, 2):
        first, second = slots[j], slots[j + 1]
        up = dot_tn(pair_cols((own, peer), first, second), grads[...]).astype(bf16)
        down = dot_tn(pair_cols((active,), first, second), g).astype(bf16)
        for i in range(2):
            rows = slice(LANES * i, LANES * (i + 1))
            split_outputs(outs, j + i, 0, up[rows])
            split_outputs(outs, j + i, LANES, down[rows])


def feed_weight(slots, own, peer, grads, gown, gpeer, active):
    half, width = own.shape
    return kernel_call(
        feed_weight_kernel,
        [SMEM] + [VMEM] * 6,
        chunk_shapes(2 * LANES, width),
        (slots, own, peer, grads, gown, gpeer, active),
        flops=8 * half * width * width,
        moved=8 << 20,
    )


def norm_rows(resid):
    average = jnp.mean(resid, axis=1, keepdims=True)
    centred = resid - average
    variance = jnp.mean(centred * centred, axis=1, keepdims=True)
    inverse = lax.rsqrt(variance + norm_eps)
    return centred * inverse, inverse


def norm_back_rows(grad_out, normed, inverse, gain):
    scaled = grad_out * gain
    return inverse * (
        scaled
        - jnp.mean(scaled, axis=1, keepdims=True)
        - normed * jnp.mean(scaled * normed, axis=1, keepdims=True)
    )


def add_sums(sums, first, grad_branch, grad_out, normed):
    terms = [grad_branch.astype(f32), grad_out * normed, grad_out]
    for row, term in enumerate(terms):
        total = jnp.sum(term, axis=0, keepdims=True)
        sums[row : row + 1, :] = total if first else sums[row : row + 1, :] + total


def norm_kernel(prev, mine, theirs, tail, out, normed, inverse):
    step = LANES
    for r in range(prev.shape[0] // step):
        rows = slice(step * r, step * (r + 1))
        branch = mine[rows].astype(f32) + theirs[rows].astype(f32) + tail[0:1]
        value, inv = norm_rows(prev[rows].astype(f32) + branch)
        normed[rows] = value
        inverse[rows] = jnp.broadcast_to(inv, (step, LANES))
        out[rows] = (value * tail[1:2] + tail[2:3]).astype(bf16)


def norm(prev, mine, theirs, tail):
    half, width = prev.shape
    return kernel_call(
        norm_kernel,
        [VMEM] * 4,
        [shape_of((half, width), bf16), shape_of((half, width), f32), shape_of((half, LANES), f32)],
        (prev, mine, theirs, tail),
        flops=20 * half * width,
        moved=4 << 20,
    )


def turn_kernel(prev, mine, theirs, tail, cot, out, grad_resid, grad_branch, sums):
    step = LANES
    for r in range(prev.shape[0] // step):
        rows = slice(step * r, step * (r + 1))
        branch = mine[rows].astype(f32) + theirs[rows].astype(f32) + tail[0:1]
        value, inv = norm_rows(prev[rows].astype(f32) + branch)
        out[rows] = (value * tail[1:2] + tail[2:3]).astype(bf16)
        grad_out = cot[rows].astype(f32)
        grad = norm_back_rows(grad_out, value, inv, tail[1:2])
        low = grad.astype(bf16)
        grad_resid[rows] = grad
        grad_branch[rows] = low
        add_sums(sums, r == 0, low, grad_out, value)


def turn(prev, mine, theirs, tail, cot):
    half, width = prev.shape
    return kernel_call(
        turn_kernel,
        [VMEM] * 5,
        [
            shape_of((half, width), bf16),
            shape_of((half, width), f32),
            shape_of((half, width), bf16),
            shape_of((8, width), f32),
        ],
        (prev, mine, theirs, tail, cot),
        flops=40 * half * width,
        moved=5 << 20,
    )


def norm_back_kernel(above, mine, theirs, normed, inverse, tail, grad_resid, grad_branch, sums):
    step = LANES
    for r in range(above.shape[0] // step):
        rows = slice(step * r, step * (r + 1))
        grad_in = above[rows] + (mine[rows].astype(f32) + theirs[rows].astype(f32))
        grad_out = grad_in.astype(bf16).astype(f32)
        value = normed[rows]
        grad = norm_back_rows(grad_out, value, inverse[rows, 0:1], tail[1:2])
        low = grad.astype(bf16)
        grad_resid[rows] = grad
        grad_branch[rows] = low
        add_sums(sums, r == 0, low, grad_out, value)


def norm_back(above, mine, theirs, normed, inverse, tail):
    half, width = above.shape
    return kernel_call(
        norm_back_kernel,
        [VMEM] * 6,
        [shape_of((half, width), f32), shape_of((half, width), bf16), shape_of((8, width), f32)],
        (above, mine, theirs, normed, inverse, tail),
        flops=30 * half * width,
        moved=5 << 20,
    )


def over_section(value, r, sources=range(SECTIONS), targets=range(SECTIONS)):
    route = [(i, i ^ r) for i in range(SECTIONS) if i in sources and (i ^ r) in targets]
    return lax.ppermute(value, "section", route)


def ring_of(n):
    return list(range(0, n, 2)) + list(range(n - 1, 0, -2))


def around(value, way):
    ring = ring_of(lax.axis_size("batch"))
    n = len(ring)
    return lax.ppermute(value, "batch", [(ring[i], ring[(i + way) % n]) for i in range(n)])


def ring_gather(shard):
    out, right, left = [shard], shard, shard
    for _ in range(3):
        right, left = around(right, 1), around(left, -1)
        out += [right, left]
    mid = shard.shape[0] // 2
    return out + [around(right[:mid], 1), around(left[mid:], -1)]


def ring_reduce(chunks):
    mid = chunks[4].shape[0]
    right, left = around(chunks[4], 1), around(chunks[8], -1)
    right = jnp.concatenate([chunks[3][:mid] + right, chunks[3][mid:]], axis=0)
    left = jnp.concatenate([chunks[5][:mid], chunks[5][mid:] + left], axis=0)
    for i in range(2):
        right = around(right, 1) + chunks[2 - i]
        left = around(left, -1) + chunks[6 + i]
    right, left = around(right, 1), around(left, -1)
    return chunks[0].astype(f32) + right.astype(f32) + left.astype(f32)


def ring_tables():
    ring = ring_of(BLOCKS)
    place = [ring.index(b) for b in range(BLOCKS)]
    steps = [0, -1, 1, -2, 2, -3, 3, 4]
    order = [[ring[(place[b] + k) % BLOCKS] for k in steps] for b in range(BLOCKS)]
    slots = [[ring[(place[b] + j) % BLOCKS] for j in range(BLOCKS)] for b in range(BLOCKS)]
    return order, slots


def double_gather(value, axis, dim):
    size, index = lax.axis_size(axis), lax.axis_index(axis)
    step = 1
    while step < size:
        other = lax.ppermute(value, axis, [(i, i ^ step) for i in range(size)])
        lower = (index // step) % 2 == 0
        value = jnp.where(
            lower,
            jnp.concatenate([value, other], axis=dim),
            jnp.concatenate([other, value], axis=dim),
        )
        step *= 2
    return value


def halve_reduce(value, axis, dim):
    size, index = lax.axis_size(axis), lax.axis_index(axis)
    step = size // 2
    while step >= 1:
        low, high = jnp.split(value, 2, axis=dim)
        lower = (index // step) % 2 == 0
        send, keep = jnp.where(lower, high, low), jnp.where(lower, low, high)
        value = keep + lax.ppermute(send, axis, [(i, i ^ step) for i in range(size)])
        step //= 2
    return value


def spread(parts, section_id, first):
    stacked = parts
    sources = (first, first + 2)
    pieces = [lax.dynamic_index_in_dim(stacked, section_id, 0, keepdims=False)]
    for r in (1, 2, 3):
        piece = lax.dynamic_index_in_dim(stacked, section_id ^ r, 0, keepdims=False)
        pieces.append(over_section(piece, r, sources=sources))
    return [lax.select_n(section_id ^ k, *pieces) for k in sources]


def collect(values, section_id, targets):
    def pick(k):
        result = values[targets[0]]
        for t in targets[1:]:
            result = jnp.where(k == t, values[t], result)
        return result

    pieces = [pick(section_id)]
    for r in (1, 2, 3):
        pieces.append(over_section(pick(section_id ^ r), r, targets=targets))
    return [lax.select_n(section_id ^ s, *pieces) for s in range(SECTIONS)]


def local(inputs, segments, timestep, weight_in, weight_out, vectors, cotangent):
    section_id = lax.axis_index("section")
    batch_id = lax.axis_index("batch")
    batch = lax.axis_size("batch")
    ringed = batch == BLOCKS
    core_id = section_id % 2
    seqs, length, width = inputs.shape
    half = seqs * length // 2
    hidden_width = weight_in.shape[2]
    unit = hidden_width // batch // SECTIONS

    if ringed:
        order_table, slot_table = ring_tables()
        order = jnp.asarray(order_table, jnp.int32)[batch_id]
        slots = jnp.asarray(slot_table, jnp.int32)[batch_id]
    else:
        order = slots = jnp.arange(BLOCKS, dtype=jnp.int32)

    def halves(value):
        rest = value.shape[2:]
        split = value.reshape((seqs, 2, 2, length // 4) + rest)
        split = jnp.moveaxis(split, 2, 0)
        return split.reshape((2, seqs, length // 2) + rest)

    def own_half(value):
        return lax.dynamic_index_in_dim(value, core_id, 0, keepdims=False)

    def peer_half(value):
        return lax.dynamic_index_in_dim(value, 1 - core_id, 0, keepdims=False)

    rows = weight_in.shape[1]
    by_head = weight_in[0].reshape(rows, -1, SECTIONS, LANES).transpose(2, 0, 1, 3)
    by_head = by_head.reshape(SECTIONS, rows, width)
    if unit == LANES:
        by_unit = by_head
    else:
        by_unit = weight_in[0].reshape(rows, -1, SECTIONS, unit).transpose(2, 0, 1, 3)
        by_unit = by_unit.reshape(SECTIONS, rows, width)
    down_parts = weight_out[0].reshape(SECTIONS, unit, width)
    attn_shards = spread(by_head, section_id, 0)
    feed_shards = spread(jnp.concatenate([by_unit, down_parts], axis=1), section_id, 1)

    vector_full = double_gather(double_gather(vectors, "section", 0), "batch", 2).astype(f32)

    def gather_attn(shard):
        if ringed:
            return ring_gather(shard)
        full = lax.all_gather(shard, "batch", axis=0, tiled=True)
        blocks = list(full.reshape(BLOCKS, LANES, width))
        return blocks[:7] + [blocks[7][: LANES // 2], blocks[7][LANES // 2 :]]

    def gather_feed(shard):
        if ringed:
            return ring_gather(shard)
        up = lax.all_gather(shard[:rows], "batch", axis=0, tiled=True).reshape(BLOCKS, LANES, width)
        down = lax.all_gather(shard[rows:], "batch", axis=0, tiled=True).reshape(BLOCKS, LANES, width)
        blocks = [jnp.concatenate([up[j], down[j]], axis=0) for j in range(7)]
        return blocks + [up[7], down[7]]

    weights = [
        gather_attn(attn_shards[0]),
        gather_feed(feed_shards[0]),
        gather_attn(attn_shards[1]),
        gather_feed(feed_shards[1]),
    ]

    def head_slice(row):
        split = row.reshape(2, SECTIONS, LANES)
        return lax.dynamic_index_in_dim(split, section_id, 1, keepdims=False).reshape(1, 256)

    def unit_slice(four):
        split = four.reshape(-1, SECTIONS, unit)
        return lax.dynamic_index_in_dim(split, section_id, 1, keepdims=False).reshape(1, width)

    biases, tails = [], []
    for k in range(SECTIONS):
        v = vector_full[k]
        if k % 2 == 0:
            biases.append(
                jnp.concatenate([head_slice(v[0]), jnp.zeros((1, 256), f32), head_slice(v[1])], axis=1)
            )
        else:
            biases.append(unit_slice(v[0:4]))
        tails.append(jnp.concatenate([v[4:7], jnp.zeros((5, width), f32)], axis=0))

    scale = timestep.astype(f32) / STEPS
    split_inputs = halves(inputs)
    embedding = scale[:, None, None] * vector_full[0, 2] + vector_full[0, 3]
    hidden = (own_half(split_inputs).astype(f32) + embedding).reshape(half, width)
    own = hidden.astype(bf16)
    peer = (peer_half(split_inputs).astype(f32) + embedding).astype(bf16).reshape(half, width)
    split_segments = halves(segments)
    seg = jnp.concatenate([own_half(split_segments), peer_half(split_segments)], axis=1).astype(f32)
    cot = own_half(halves(cotangent)).reshape(half, width)

    def exchange(p_own, p_send):
        mine = (p_own + over_section(p_send, 1).astype(f32)).astype(bf16)
        return mine, over_section(mine, 2)

    def to_all(packed):
        return lax.all_to_all(packed, "section", 0, 0)

    saved = []
    prev = hidden
    for k in range(SECTIONS):
        if k % 2 == 0:
            wo = to_all(pack_out(order, weights[k]))
            qkv, probs, ctx = attend(order, own, peer, seg, biases[k], weights[k])
            p_own, p_send = project(ctx, wo, width)
            kept = (own, peer, wo, qkv, probs, ctx)
        else:
            p_own, p_send, active, slope = feed(order, own, peer, biases[k], weights[k])
            kept = (own, peer, active, slope)
        mine, theirs = exchange(p_own, p_send)
        if k < SECTIONS - 1:
            out, normed, inverse = norm(prev, mine, theirs, tails[k])
            saved.append((kept, normed, inverse))
            prev, own, peer = out, out, over_section(out, 1)
        else:
            out, grad_resid, grad_own, tail_sums = turn(prev, mine, theirs, tails[k], cot)
            saved.append((kept, None, None))

    pick_rows = lax.dynamic_index_in_dim(
        out.reshape(seqs, 2, length // 4, width), section_id // 2, 1, keepdims=False
    )

    shards, vector_terms = [None] * SECTIONS, [None] * SECTIONS
    for k in range(SECTIONS - 1, -1, -1):
        kept, _, _ = saved[k]
        grad_peer = over_section(grad_own, 1)
        if k % 2 == 0:
            own, peer, wo, qkv, probs, ctx = kept
            wo_grad = to_all(out_grad(grad_own, grad_peer, ctx))
            p_own, p_send, grads, sums = attend_back(
                order, grad_own, grad_peer, wo, qkv, probs, weights[k]
            )
            chunks = attend_weight(slots, own, peer, grads, wo_grad)

            def placed(piece):
                empty = jnp.zeros((2, SECTIONS, LANES), f32)
                piece = piece.reshape(2, 1, LANES)
                return lax.dynamic_update_slice_in_dim(empty, piece, section_id, 1).reshape(1, width)

            head = [placed(sums[0, :256]), placed(sums[0, 512:])]
        else:
            own, peer, active, slope = kept
            p_own, p_send, grads, sums = feed_back(order, grad_own, grad_peer, slope, weights[k])
            chunks = feed_weight(slots, own, peer, grads, grad_own, grad_peer, active)
            empty = jnp.zeros((width // unit, SECTIONS, unit), f32)
            piece = sums[0].reshape(width // unit, 1, unit)
            head = [lax.dynamic_update_slice_in_dim(empty, piece, section_id, 1).reshape(4, width)]
        shards[k] = chunks
        tail = 0.5 * tail_sums[:3]
        mine, theirs = exchange(p_own, p_send)
        if k > 0:
            _, normed, inverse = saved[k - 1]
            above = grad_resid
            grad_resid, grad_own, tail_sums = norm_back(
                above, mine, theirs, normed, inverse, tails[k - 1]
            )
            middle = [jnp.zeros((2, width), f32)] if k == 2 else []
        else:
            input_grad = grad_resid + (mine.astype(f32) + theirs.astype(f32))
            per_sequence = jnp.sum(input_grad.reshape(seqs, length // 2, width), axis=1)
            middle = [
                0.5 * jnp.sum(scale[:, None] * per_sequence, axis=0, keepdims=True),
                0.5 * jnp.sum(per_sequence, axis=0, keepdims=True),
            ]
        vector_terms[k] = jnp.concatenate(head + middle + [tail], axis=0)

    input_part = lax.dynamic_index_in_dim(
        input_grad.reshape(seqs, 2, length // 4, width), section_id // 2, 1, keepdims=False
    )

    def reduce_chunks(k):
        chunks = list(shards[k])
        if ringed:
            total = ring_reduce(chunks).astype(bf16)
            return (total, None) if k % 2 == 0 else (total[:rows], total[rows:])

        def scatter(parts):
            return lax.psum_scatter(
                jnp.concatenate(parts, axis=0), "batch", scatter_dimension=0, tiled=True
            )

        if k % 2 == 0:
            blocks = chunks[:4] + [chunks[4], chunks[8]] + chunks[5:8]
            return scatter(blocks), None
        up = [c[:LANES] for c in chunks[:4]] + [chunks[4]] + [c[:LANES] for c in chunks[5:8]]
        down = [c[LANES:] for c in chunks[:4]] + [chunks[8]] + [c[LANES:] for c in chunks[5:8]]
        return scatter(up), scatter(down)

    reduced = [None] * SECTIONS
    for k in range(SECTIONS - 1, -1, -1):
        reduced[k] = reduce_chunks(k)

    slices = collect([r[0] for r in reduced], section_id, list(range(SECTIONS)))
    first = jnp.stack([p.reshape(rows, -1, LANES) for p in slices], axis=2)
    first = first.reshape(rows, hidden_width)
    if unit != LANES:
        other = jnp.stack([p.reshape(rows, -1, unit) for p in slices], axis=2)
        first = jnp.where(section_id % 2 == 1, other.reshape(rows, hidden_width), first)
    second = jnp.stack(collect([r[1] for r in reduced], section_id, [1, 3]), axis=0)
    second = second.reshape(SECTIONS * unit, width).astype(f32)
    second = jnp.where(section_id % 2 == 1, second, 0.0)

    terms = jnp.stack(vector_terms)
    terms = halve_reduce(halve_reduce(terms, "section", 0), "batch", 2)
    return (pick_rows, input_part, first.astype(f32)[None], second[None], terms)


def solution(mesh):
    return jax.shard_map(
        local,
        mesh=mesh,
        in_specs=(
            P("batch", None, None),
            P("batch", None),
            P("batch"),
            P("section", "batch", None),
            P("section", "batch", None),
            P("section", None, "batch"),
            P("batch", None, None),
        ),
        out_specs=(
            P("batch", "section", None),
            P("batch", "section", None),
            P("section", "batch", None),
            P("section", "batch", None),
            P("section", None, "batch"),
        ),
        check_vma=False,
    )
```

time: 1450 us -> 513 us (0.35)
  the two profiles are of different devices: /device:TPU:0 before, /device:TPU:1 now
where the time goes in v1:
time: 513 us; the launch traced here: 503 us
  waiting for transfers between devices  165 us (32%)
  starting transfers between devices  141 us (27%)
  Pallas kernels  74.8 us (15%)
  local copies, waits for them, and re-layouts  68.3 us (13%)
  other arithmetic  50.7 us (10%)
    ppermute x64, waiting for transfers between devices, around(): lax.ppermute(value, 'batch', [(ring[i], ring[(i + way) % n]) for i in ran...  96.3 us
    pallas_call x25, Pallas kernels, kernel_call(): pl.pallas_call(body, in_specs=in_specs, out_specs=[VMEM] * len(outs), out...  74.8 us
    ppermute x35, starting transfers between devices, over_section(): return lax.ppermute(value, 'section', route)  59.9 us
    ppermute x64, starting transfers between devices, around(): lax.ppermute(value, 'batch', [(ring[i], ring[(i + way) % n]) for i in ran...  48.3 us
    unnamed x357, local copies, waits for them, and re-layouts  44 us
    ppermute x35, waiting for transfers between devices, over_section(): return lax.ppermute(value, 'section', route)  40.7 us
    all_to_all x4, starting transfers between devices, to_all(): return lax.all_to_all(packed, 'section', 0, 0)  20.4 us
    ppermute x5, waiting for transfers between devices, double_gather(): other = lax.ppermute(value, axis, [(i, i ^ step) for i in range(size)])  14.5 us
  transfers between devices with their start and end apart: 113, of which 46 were waited for; matrix products, arithmetic and copies ran while one was open for 14% of the time, Pallas kernels for 11%

profile of v1, /device:TPU:1, one launch (start us, length us, event | category | flops | bytes accessed | tf_op | source)
XLA Modules:
  0.0 503.4 jit_solution(252882337552759679)
XLA Ops:
  9.5 4.6 collective-permute-start.20
  15.6 8.4 %collective-permute-done.1 = bf16[2,7,128]{2,1,0:T(8,128)(2,1)S(1)} collective-permute-done((bf16[2,7,128]{2,1,0:T(8,128)(2,1)S(1)}, bf16[2,7,128]{2,1,0:T(8,128)(2,1)S(1)}, u32[]{:S(2)}, u32[]{:S(2)}) %collective-permute-start.1) | collective-permute-done | bytes 3616 | tf_op jit(solution)/shard_map/ppermute | solution.py:665
  24.1 2.6 collective-permute-start.21
  32.1 3.7 collective-permute-done.8.refs_1_
  40.8 5.9 %collective-permute-done.4 = bf16[4,7,512]{2,1,0:T(8,128)(2,1)S(1)} collective-permute-done((bf16[4,7,512]{2,1,0:T(8,128)(2,1)S(1)}, bf16[4,7,512]{2,1,0:T(8,128)(2,1)S(1)}, u32[]{:S(2)}, u32[]{:S(2)}) %collective-permute-start.4) | collective-permute-done | bytes 28704 | tf_op jit(solution)/shard_map/ppermute | solution.py:665
  50.7 5.8 %collective-permute-done.12.refs_5_ = bf16[128,1024]{1,0:T(8,128)(2,1)S(1)} collective-permute-done((bf16[128,1024]{1,0:T(8,128)(2,1)S(1)}, bf16[128,1024]{1,0:T(8,128)(2,1)S(1)}, u32[]{:S(2)}, u32[]{:S(2)}) %collective-permute-start.12) | collective-permute-done | bytes 262176 | tf_op jit(solution)/shard_map/ppermute | solution.py:628
  58.1 3.9 collective-permute-done.14.refs_7_
  64.3 5.0 all-to-all-start
  71.1 3.0 select_select_fusion
  75.6 4.3 shard_map.128
  90.7 10.0 %collective-permute-done.24.refs_3_ = bf16[256,1024]{1,0:T(8,128)(2,1)S(1)} collective-permute-done((bf16[256,1024]{1,0:T(8,128)(2,1)}, bf16[256,1024]{1,0:T(8,128)(2,1)S(1)}, u32[]{:S(2)}, u32[]{:S(2)}) %collective-permute-start.24) | collective-permute-done | bytes 524320 | tf_op jit(solution)/shard_map/ppermute | solution.py:628
  107.5 4.9 collective-permute-done.26.refs_5_
  119.3 2.4 collective-permute-done.29.refs_8_
  126.0 5.7 %shard_map.132 = (f32[256,1024]{1,0:T(8,128)S(1)}, bf16[256,1024]{1,0:T(8,128)(2,1)S(1)}, bf16[512,1024]{1,0:T(8,128)(2,1)S(1)}, f32[512,1024]{1,0:T(8,128)S(1)}) custom-call(s32[8]{0:T(128)S(1)} %fusion.22.order, bf16[256,1024]{1,0:T(8,128)(2,1)} %get-tuple-element.100.own.prev, bf16[256,1024]{1,0:T(8,128)(2,1)S(1)} %collective-permute-done.18.peer, ...), custom_call_target="tpu_custom_call" | custom-call | flops 2147483648 | bytes 10485760 | tf_op jit(solution)/shard_map/pallas_call | solution.py:43
  134.2 3.7 collective-permute-start.30
  140.5 5.3 %collective-permute-done.33.refs_1_ = bf16[128,1024]{1,0:T(8,128)(2,1)S(1)} collective-permute-done((bf16[128,1024]{1,0:T(8,128)(2,1)S(1)}, bf16[128,1024]{1,0:T(8,128)(2,1)S(1)}, u32[]{:S(2)}, u32[]{:S(2)}) %collective-permute-start.33) | collective-permute-done | bytes 262176 | tf_op jit(solution)/shard_map/ppermute | solution.py:628
  147.3 5.6 %collective-permute-done.35.refs_3_ = bf16[128,1024]{1,0:T(8,128)(2,1)S(1)} collective-permute-done((bf16[128,1024]{1,0:T(8,128)(2,1)S(1)}, bf16[128,1024]{1,0:T(8,128)(2,1)S(1)}, u32[]{:S(2)}, u32[]{:S(2)}) %collective-permute-start.35) | collective-permute-done | bytes 262176 | tf_op jit(solution)/shard_map/ppermute | solution.py:628
  166.9 7.2 %all-to-all-start.1 = ((bf16[4,2,128,256]{3,2,1,0:T(8,128)(2,1)}), bf16[4,2,128,256]{3,2,1,0:T(8,128)(2,1)}, u32[]{:S(2)}, u32[]{:S(2)}) async-start(bf16[4,2,128,256]{3,2,1,0:T(8,128)(2,1)} %copy-done.11), calls=%async_computation.1 | async-start | bytes 1048576 | tf_op jit(solution)/shard_map/all_to_all | solution.py:811
  178.3 4.9 shard_map.134
  192.7 10.3 %collective-permute-done.46.refs_3_ = bf16[256,1024]{1,0:T(8,128)(2,1)S(1)} collective-permute-done((bf16[256,1024]{1,0:T(8,128)(2,1)}, bf16[256,1024]{1,0:T(8,128)(2,1)S(1)}, u32[]{:S(2)}, u32[]{:S(2)}) %collective-permute-start.46) | collective-permute-done | bytes 524320 | tf_op jit(solution)/shard_map/ppermute | solution.py:628
  210.0 5.6 %collective-permute-done.48.refs_5_ = bf16[256,1024]{1,0:T(8,128)(2,1)S(1)} collective-permute-done((bf16[256,1024]{1,0:T(8,128)(2,1)S(1)}, bf16[256,1024]{1,0:T(8,128)(2,1)S(1)}, u32[]{:S(2)}, u32[]{:S(2)}) %collective-permute-start.48) | collective-permute-done | bytes 524320 | tf_op jit(solution)/shard_map/ppermute | solution.py:628
  223.5 2.6 collective-permute-done.51.refs_8_
  231.4 5.7 %shard_map.138 = (f32[256,1024]{1,0:T(8,128)S(1)}, bf16[256,1024]{1,0:T(8,128)(2,1)S(1)}, bf16[512,1024]{1,0:T(8,128)(2,1)S(1)}, f32[512,1024]{1,0:T(8,128)S(1)}) custom-call(s32[8]{0:T(128)S(1)} %fusion.22.order, bf16[256,1024]{1,0:T(8,128)(2,1)} %get-tuple-element.107.own.prev, bf16[256,1024]{1,0:T(8,128)(2,1)} %collective-permute-done.43.peer, ...), custom_call_target="tpu_custom_call" | custom-call | flops 2147483648 | bytes 10485760 | tf_op jit(solution)/shard_map/pallas_call | solution.py:43
  237.1 3.0 collective-permute-start.52
  243.7 11.7 %collective-permute-done.53.theirs = bf16[256,1024]{1,0:T(8,128)(2,1)S(1)} collective-permute-done((bf16[256,1024]{1,0:T(8,128)(2,1)S(1)}, bf16[256,1024]{1,0:T(8,128)(2,1)S(1)}, u32[]{:S(2)}, u32[]{:S(2)}) %collective-permute-start.53) | collective-permute-done | bytes 524320 | tf_op jit(solution)/shard_map/ppermute | solution.py:618
  261.0 4.5 shard_map.140
  269.8 3.7 shard_map.147
  275.8 5.0 collective-permute-done.56.theirs
  286.5 7.0 %shard_map.142 = (f32[256,1024]{1,0:T(8,128)S(1)}, bf16[256,1024]{1,0:T(8,128)(2,1)}, bf16[512,768]{1,0:T(8,128)(2,1)S(1)}, f32[8,768]{1,0:T(8,128)S(1)}) custom-call(s32[8]{0:T(128)S(1)} %fusion.22.order, bf16[256,1024]{1,0:T(8,128)(2,1)S(1)} %get-tuple-element.119.own, bf16[256,1024]{1,0:T(8,128)(2,1)S(1)} %collective-permute-done.57.peer, ...), custom_call_target="tpu_custom_call" | custom-call | flops 1073741824 | bytes 8388608 | tf_op jit(solution)/shard_map/pallas_call | solution.py:43
  308.5 4.7 all-to-all-start.2
  325.2 2.6 shard_map.149
  329.9 2.6 collective-permute-done.59.theirs
  338.6 4.4 shard_map.144
  344.9 3.5 shard_map.150
  350.3 5.8 %collective-permute-done.86 = bf16[128,1024]{1,0:T(8,128)(2,1)S(1)} collective-permute-done((bf16[128,1024]{1,0:T(8,128)(2,1)S(1)}, bf16[128,1024]{1,0:T(8,128)(2,1)S(1)}, u32[]{:S(2)}, u32[]{:S(2)}) %collective-permute-start.86) | collective-permute-done | bytes 262176 | tf_op jit(solution)/shard_map/ppermute | solution.py:628
  359.6 3.3 collective-permute-done.62.theirs
  367.1 2.6 collective-permute-done.87
  375.3 6.9 %shard_map.146 = (f32[256,1024]{1,0:T(8,128)S(1)}, bf16[256,1024]{1,0:T(8,128)(2,1)}, bf16[512,768]{1,0:T(8,128)(2,1)S(1)}, f32[8,768]{1,0:T(8,128)S(1)}) custom-call(s32[8]{0:T(128)S(1)} %fusion.22.order, bf16[256,1024]{1,0:T(8,128)(2,1)S(1)} %get-tuple-element.134.own, bf16[256,1024]{1,0:T(8,128)(2,1)S(1)} %collective-permute-done.63.peer, ...), custom_call_target="tpu_custom_call" | custom-call | flops 1073741824 | bytes 8388608 | tf_op jit(solution)/shard_map/pallas_call | solution.py:43
  388.4 3.6 all-to-all-start.3
  393.4 6.6 %all-to-all-done.3.wo_grad = bf16[4,2,128,256]{3,2,1,0:T(8,128)(2,1)S(1)} async-done(((bf16[4,2,128,256]{3,2,1,0:T(8,128)(2,1)}), bf16[4,2,128,256]{3,2,1,0:T(8,128)(2,1)S(1)}, u32[]{:S(2)}, u32[]{:S(2)}) %all-to-all-start.3) | async-done | bytes 524320 | tf_op jit(solution)/shard_map/all_to_all | solution.py:811
  411.2 9.4 %collective-permute-done.65 = bf16[256,1024]{1,0:T(8,128)(2,1)S(1)} collective-permute-done((bf16[256,1024]{1,0:T(8,128)(2,1)S(1)}, bf16[256,1024]{1,0:T(8,128)(2,1)S(1)}, u32[]{:S(2)}, u32[]{:S(2)}) %collective-permute-start.65) | collective-permute-done | bytes 524320 | tf_op jit(solution)/shard_map/ppermute | solution.py:618
  428.1 4.0 collective-permute-start.105
  443.3 3.2 collective-permute-done.80
  450.0 13.2 %collective-permute-done.96 = bf16[128,1024]{1,0:T(8,128)(2,1)S(1)} collective-permute-done((bf16[128,1024]{1,0:T(8,128)(2,1)S(1)}, bf16[128,1024]{1,0:T(8,128)(2,1)S(1)}, u32[]{:S(2)}, u32[]{:S(2)}) %collective-permute-start.96) | collective-permute-done | bytes 262176 | tf_op jit(solution)/shard_map/ppermute | solution.py:628
  467.2 6.9 %collective-permute-done.107 = f32[1,7,256]{2,1,0:T(8,128)S(1)} collective-permute-done((f32[1,7,256]{2,1,0:T(8,128)S(1)}, f32[1,7,256]{2,1,0:T(8,128)S(1)}, u32[]{:S(2)}, u32[]{:S(2)}) %collective-permute-start.107) | collective-permute-done | bytes 7200 | tf_op jit(solution)/shard_map/ppermute | solution.py:683
  477.4 6.5 %collective-permute-start.100 = (bf16[128,1024]{1,0:T(8,128)(2,1)S(1)}, bf16[128,1024]{1,0:T(8,128)(2,1)S(1)}, u32[]{:S(2)}, u32[]{:S(2)}) collective-permute-start(bf16[128,1024]{1,0:T(8,128)(2,1)S(1)} %get-tuple-element.210), channel_id=1, source_target_pairs={{0,24},{8,16},{16,8},{24,0},{1,25},{9,17},{17,9},{25,1},{2,26},{10... | collective-permute-start | bytes 786440 | tf_op jit(solution)/shard_map/ppermute | solution.py:618
  483.9 2.4 collective-permute-start.102
  492.4 3.6 collective-permute-done.102
  (706 shorter events, 248.6 us)
Async XLA Ops:
  0.6 13.7 %collective-permute-start = (bf16[1,7,128]{2,1,0:T(8,128)(2,1)}, bf16[1,7,128]{2,1,0:T(8,128)(2,1)S(1)}, u32[]{:S(2)}, u32[]{:S(2)}) collective-permute-start(bf16[1,7,128]{2,1,0:T(8,128)(2,1)} %param.14), channel_id=1, source_target_pairs={{0,8},{8,0},{16,24},{24,16},{1,9},{9,1},{17,25},{25,17},{2,10},{10... | collective-permute-start | bytes 5384 | tf_op jit(solution)/shard_map/ppermute | solution.py:665
  4.2 22.5 %collective-permute-start.5 = (bf16[128,1024]{1,0:T(8,128)(2,1)}, bf16[128,1024]{1,0:T(8,128)(2,1)S(1)}, u32[]{:S(2)}, u32[]{:S(2)}) collective-permute-start(bf16[128,1024]{1,0:T(8,128)(2,1)} %get-tuple-element.225), channel_id=1, source_target_pairs={{0,8},{16,24},{1,9},{17,25},{2,10},{18,26},{3,11},{19,27},{4,12},{... | collective-permute-start | bytes 786440 | tf_op jit(solution)/shard_map/ppermute | solution.py:618
  5.6 22.4 %collective-permute-start.6 = (bf16[128,1024]{1,0:T(8,128)(2,1)}, bf16[128,1024]{1,0:T(8,128)(2,1)}, u32[]{:S(2)}, u32[]{:S(2)}) collective-permute-start(bf16[128,1024]{1,0:T(8,128)(2,1)} %get-tuple-element.224), channel_id=1, source_target_pairs={{0,16},{16,0},{1,17},{17,1},{2,18},{18,2},{3,19},{19,3},{4,20},{20... | collective-permute-start | bytes 786440 | tf_op jit(solution)/shard_map/ppermute | solution.py:618
  7.0 21.0 %collective-permute-start.7 = (bf16[128,1024]{1,0:T(8,128)(2,1)}, bf16[128,1024]{1,0:T(8,128)(2,1)}, u32[]{:S(2)}, u32[]{:S(2)}) collective-permute-start(bf16[128,1024]{1,0:T(8,128)(2,1)} %get-tuple-element.223), channel_id=1, source_target_pairs={{0,24},{16,8},{1,25},{17,9},{2,26},{18,10},{3,27},{19,11},{4,28},{... | collective-permute-start | bytes 786440 | tf_op jit(solution)/shard_map/ppermute | solution.py:618
  9.5 61.4 %collective-permute-start.20 = (bf16[256,1024]{1,0:T(8,128)(2,1)}, bf16[256,1024]{1,0:T(8,128)(2,1)}, u32[]{:S(2)}, u32[]{:S(2)}) collective-permute-start(bf16[256,1024]{1,0:T(8,128)(2,1)} %get-tuple-element.206), channel_id=1, source_target_pairs={{8,24},{24,8},{9,25},{25,9},{10,26},{26,10},{11,27},{27,11},{12,28... | collective-permute-start | bytes 1572872 | tf_op jit(solution)/shard_map/ppermute | solution.py:618
  24.1 46.9 %collective-permute-start.21 = (bf16[256,1024]{1,0:T(8,128)(2,1)}, bf16[256,1024]{1,0:T(8,128)(2,1)}, u32[]{:S(2)}, u32[]{:S(2)}) collective-permute-start(bf16[256,1024]{1,0:T(8,128)(2,1)} %get-tuple-element.207), channel_id=1, source_target_pairs={{8,16},{24,0},{9,17},{25,1},{10,18},{26,2},{11,19},{27,3},{12,20},... | collective-permute-start | bytes 1572872 | tf_op jit(solution)/shard_map/ppermute | solution.py:618
  35.8 13.3 %collective-permute-start.10 = (bf16[128,1024]{1,0:T(8,128)(2,1)S(1)}, bf16[128,1024]{1,0:T(8,128)(2,1)S(1)}, u32[]{:S(2)}, u32[]{:S(2)}) collective-permute-start(bf16[128,1024]{1,0:T(8,128)(2,1)S(1)} %collective-permute-done.8.refs_1_), channel_id=1, source_target_pairs={{0,2},{2,4},{4,6},{6,7},{7,5},{5,3},{3,1},{1,0},{8,10},{10,12},{12... | collective-permute-start | bytes 786440 | tf_op jit(solution)/shard_map/ppermute | solution.py:628
  46.7 24.3 %collective-permute-start.19 = (bf16[256,1024]{1,0:T(8,128)(2,1)}, bf16[256,1024]{1,0:T(8,128)(2,1)}, u32[]{:S(2)}, u32[]{:S(2)}) collective-permute-start(bf16[256,1024]{1,0:T(8,128)(2,1)} %get-tuple-element.205), channel_id=1, source_target_pairs={{8,0},{24,16},{9,1},{25,17},{10,2},{26,18},{11,3},{27,19},{12,4},{... | collective-permute-start | bytes 1572872 | tf_op jit(solution)/shard_map/ppermute | solution.py:618
  64.3 18.5 %all-to-all-start = ((bf16[4,2,128,256]{3,2,1,0:T(8,128)(2,1)}), bf16[4,2,128,256]{3,2,1,0:T(8,128)(2,1)}, u32[]{:S(2)}, u32[]{:S(2)}) async-start(bf16[4,2,128,256]{3,2,1,0:T(8,128)(2,1)} %shard_map.129), calls=%async_computation | async-start | bytes 1048576 | tf_op jit(solution)/shard_map/all_to_all | solution.py:811
  74.2 13.8 %collective-permute-start.22 = (bf16[256,1024]{1,0:T(8,128)(2,1)}, bf16[256,1024]{1,0:T(8,128)(2,1)}, u32[]{:S(2)}, u32[]{:S(2)}) collective-permute-start(bf16[256,1024]{1,0:T(8,128)(2,1)} %get-tuple-element.204.refs_0_), channel_id=1, source_target_pairs={{0,2},{2,4},{4,6},{6,7},{7,5},{5,3},{3,1},{1,0},{8,10},{10,12},{12... | collective-permute-start | bytes 1572872 | tf_op jit(solution)/shard_map/ppermute | solution.py:628
  74.2 13.9 %collective-permute-start.23 = (bf16[256,1024]{1,0:T(8,128)(2,1)}, bf16[256,1024]{1,0:T(8,128)(2,1)}, u32[]{:S(2)}, u32[]{:S(2)}) collective-permute-start(bf16[256,1024]{1,0:T(8,128)(2,1)} %get-tuple-element.204.refs_0_), channel_id=1, source_target_pairs={{0,1},{2,0},{4,2},{6,4},{7,6},{5,7},{3,5},{1,3},{8,9},{10,8},{12,1... | collective-permute-start | bytes 1572872 | tf_op jit(solution)/shard_map/ppermute | solution.py:628
  89.6 13.3 %collective-permute-start.17 = (bf16[256,1024]{1,0:T(8,128)(2,1)S(1)}, bf16[256,1024]{1,0:T(8,128)(2,1)S(1)}, u32[]{:S(2)}, u32[]{:S(2)}) collective-permute-start(bf16[256,1024]{1,0:T(8,128)(2,1)S(1)} %add_convert_fusion.9.mine), channel_id=1, source_target_pairs={{0,16},{8,24},{16,0},{24,8},{1,17},{9,25},{17,1},{25,9},{2,18},{10... | collective-permute-start | bytes 1572872 | tf_op jit(solution)/shard_map/ppermute | solution.py:618
  101.0 13.3 %collective-permute-start.27 = (bf16[256,1024]{1,0:T(8,128)(2,1)S(1)}, bf16[256,1024]{1,0:T(8,128)(2,1)S(1)}, u32[]{:S(2)}, u32[]{:S(2)}) collective-permute-start(bf16[256,1024]{1,0:T(8,128)(2,1)S(1)} %collective-permute-done.25.refs_4_), channel_id=1, source_target_pairs={{0,1},{2,0},{4,2},{6,4},{7,6},{5,7},{3,5},{1,3},{8,9},{10,8},{12,1... | collective-permute-start | bytes 1572872 | tf_op jit(solution)/shard_map/ppermute | solution.py:628
  105.2 16.6 %collective-permute-start.18 = (bf16[256,1024]{1,0:T(8,128)(2,1)}, bf16[256,1024]{1,0:T(8,128)(2,1)S(1)}, u32[]{:S(2)}, u32[]{:S(2)}) collective-permute-start(bf16[256,1024]{1,0:T(8,128)(2,1)} %get-tuple-element.100.own.prev), channel_id=1, source_target_pairs={{0,8},{8,0},{16,24},{24,16},{1,9},{9,1},{17,25},{25,17},{2,10},{10... | collective-permute-start | bytes 1572872 | tf_op jit(solution)/shard_map/ppermute | solution.py:618
  139.5 14.8 %collective-permute-start.31 = (bf16[256,1024]{1,0:T(8,128)(2,1)S(1)}, bf16[256,1024]{1,0:T(8,128)(2,1)S(1)}, u32[]{:S(2)}, u32[]{:S(2)}) collective-permute-start(bf16[256,1024]{1,0:T(8,128)(2,1)S(1)} %add_convert_fusion.8.mine), channel_id=1, source_target_pairs={{0,16},{8,24},{16,0},{24,8},{1,17},{9,25},{17,1},{25,9},{2,18},{10... | collective-permute-start | bytes 1572872 | tf_op jit(solution)/shard_map/ppermute | solution.py:618
  157.7 17.8 %collective-permute-start.32 = (bf16[256,1024]{1,0:T(8,128)(2,1)}, bf16[256,1024]{1,0:T(8,128)(2,1)}, u32[]{:S(2)}, u32[]{:S(2)}) collective-permute-start(bf16[256,1024]{1,0:T(8,128)(2,1)} %get-tuple-element.103.own.prev), channel_id=1, source_target_pairs={{0,8},{8,0},{16,24},{24,16},{1,9},{9,1},{17,25},{25,17},{2,10},{10... | collective-permute-start | bytes 1572872 | tf_op jit(solution)/shard_map/ppermute | solution.py:618
  166.9 19.3 %all-to-all-start.1 = ((bf16[4,2,128,256]{3,2,1,0:T(8,128)(2,1)}), bf16[4,2,128,256]{3,2,1,0:T(8,128)(2,1)}, u32[]{:S(2)}, u32[]{:S(2)}) async-start(bf16[4,2,128,256]{3,2,1,0:T(8,128)(2,1)} %copy-done.11), calls=%async_computation.1 | async-start | bytes 1048576 | tf_op jit(solution)/shard_map/all_to_all | solution.py:811
  174.0 15.3 %collective-permute-start.44 = (bf16[256,1024]{1,0:T(8,128)(2,1)}, bf16[256,1024]{1,0:T(8,128)(2,1)}, u32[]{:S(2)}, u32[]{:S(2)}) collective-permute-start(bf16[256,1024]{1,0:T(8,128)(2,1)} %get-tuple-element.203.refs_0_), channel_id=1, source_target_pairs={{0,2},{2,4},{4,6},{6,7},{7,5},{5,3},{3,1},{1,0},{8,10},{10,12},{12... | collective-permute-start | bytes 1572872 | tf_op jit(solution)/shard_map/ppermute | solution.py:628
  175.0 15.3 %collective-permute-start.45 = (bf16[256,1024]{1,0:T(8,128)(2,1)}, bf16[256,1024]{1,0:T(8,128)(2,1)}, u32[]{:S(2)}, u32[]{:S(2)}) collective-permute-start(bf16[256,1024]{1,0:T(8,128)(2,1)} %get-tuple-element.203.refs_0_), channel_id=1, source_target_pairs={{0,1},{2,0},{4,2},{6,4},{7,6},{5,7},{3,5},{1,3},{8,9},{10,8},{12,1... | collective-permute-start | bytes 1572872 | tf_op jit(solution)/shard_map/ppermute | solution.py:628
  189.3 13.7 %collective-permute-start.46 = (bf16[256,1024]{1,0:T(8,128)(2,1)}, bf16[256,1024]{1,0:T(8,128)(2,1)S(1)}, u32[]{:S(2)}, u32[]{:S(2)}) collective-permute-start(bf16[256,1024]{1,0:T(8,128)(2,1)} %collective-permute-done.44.refs_1_), channel_id=1, source_target_pairs={{0,2},{2,4},{4,6},{6,7},{7,5},{5,3},{3,1},{1,0},{8,10},{10,12},{12... | collective-permute-start | bytes 1572872 | tf_op jit(solution)/shard_map/ppermute | solution.py:628
  190.3 13.7 %collective-permute-start.47 = (bf16[256,1024]{1,0:T(8,128)(2,1)}, bf16[256,1024]{1,0:T(8,128)(2,1)S(1)}, u32[]{:S(2)}, u32[]{:S(2)}) collective-permute-start(bf16[256,1024]{1,0:T(8,128)(2,1)} %collective-permute-done.45.refs_2_), channel_id=1, source_target_pairs={{0,1},{2,0},{4,2},{6,4},{7,6},{5,7},{3,5},{1,3},{8,9},{10,8},{12,1... | collective-permute-start | bytes 1572872 | tf_op jit(solution)/shard_map/ppermute | solution.py:628
  191.0 13.5 %collective-permute-start.42 = (bf16[256,1024]{1,0:T(8,128)(2,1)S(1)}, bf16[256,1024]{1,0:T(8,128)(2,1)S(1)}, u32[]{:S(2)}, u32[]{:S(2)}) collective-permute-start(bf16[256,1024]{1,0:T(8,128)(2,1)S(1)} %add_convert_fusion.7.mine), channel_id=1, source_target_pairs={{0,16},{8,24},{16,0},{24,8},{1,17},{9,25},{17,1},{25,9},{2,18},{10... | collective-permute-start | bytes 1572872 | tf_op jit(solution)/shard_map/ppermute | solution.py:618
  204.0 14.1 %collective-permute-start.49 = (bf16[256,1024]{1,0:T(8,128)(2,1)S(1)}, bf16[256,1024]{1,0:T(8,128)(2,1)S(1)}, u32[]{:S(2)}, u32[]{:S(2)}) collective-permute-start(bf16[256,1024]{1,0:T(8,128)(2,1)S(1)} %collective-permute-done.47.refs_4_), channel_id=1, source_target_pairs={{0,1},{2,0},{4,2},{6,4},{7,6},{5,7},{3,5},{1,3},{8,9},{10,8},{12,1... | collective-permute-start | bytes 1572872 | tf_op jit(solution)/shard_map/ppermute | solution.py:628
  208.5 17.6 %collective-permute-start.43 = (bf16[256,1024]{1,0:T(8,128)(2,1)}, bf16[256,1024]{1,0:T(8,128)(2,1)}, u32[]{:S(2)}, u32[]{:S(2)}) collective-permute-start(bf16[256,1024]{1,0:T(8,128)(2,1)} %get-tuple-element.107.own.prev), channel_id=1, source_target_pairs={{0,8},{8,0},{16,24},{24,16},{1,9},{9,1},{17,25},{25,17},{2,10},{10... | collective-permute-start | bytes 1572872 | tf_op jit(solution)/shard_map/ppermute | solution.py:618
  241.8 13.6 %collective-permute-start.53 = (bf16[256,1024]{1,0:T(8,128)(2,1)S(1)}, bf16[256,1024]{1,0:T(8,128)(2,1)S(1)}, u32[]{:S(2)}, u32[]{:S(2)}) collective-permute-start(bf16[256,1024]{1,0:T(8,128)(2,1)S(1)} %add_convert_fusion.6.mine), channel_id=1, source_target_pairs={{0,16},{8,24},{16,0},{24,8},{1,17},{9,25},{17,1},{25,9},{2,18},{10... | collective-permute-start | bytes 1572872 | tf_op jit(solution)/shard_map/ppermute | solution.py:618
  283.9 17.5 %collective-permute-start.71 = (bf16[256,1024]{1,0:T(8,128)(2,1)}, bf16[256,1024]{1,0:T(8,128)(2,1)}, u32[]{:S(2)}, u32[]{:S(2)}) collective-permute-start(bf16[256,1024]{1,0:T(8,128)(2,1)} %pad_maximum_fusion.1), channel_id=1, source_target_pairs={{0,1},{2,0},{4,2},{6,4},{7,6},{5,7},{3,5},{1,3},{8,9},{10,8},{12,1... | collective-permute-start | bytes 1572872 | tf_op jit(solution)/shard_map/ppermute | solution.py:628
  285.4 18.8 %collective-permute-start.67 = (bf16[256,1024]{1,0:T(8,128)(2,1)}, bf16[256,1024]{1,0:T(8,128)(2,1)}, u32[]{:S(2)}, u32[]{:S(2)}) collective-permute-start(bf16[256,1024]{1,0:T(8,128)(2,1)} %pad_maximum_fusion), channel_id=1, source_target_pairs={{0,2},{2,4},{4,6},{6,7},{7,5},{5,3},{3,1},{1,0},{8,10},{10,12},{12... | collective-permute-start | bytes 1572872 | tf_op jit(solution)/shard_map/ppermute | solution.py:628
  295.5 17.7 %collective-permute-start.58 = (bf16[256,1024]{1,0:T(8,128)(2,1)}, bf16[256,1024]{1,0:T(8,128)(2,1)}, u32[]{:S(2)}, u32[]{:S(2)}) collective-permute-start(bf16[256,1024]{1,0:T(8,128)(2,1)} %get-tuple-element.123), channel_id=1, source_target_pairs={{0,8},{8,0},{16,24},{24,16},{1,9},{9,1},{17,25},{25,17},{2,10},{10... | collective-permute-start | bytes 1572872 | tf_op jit(solution)/shard_map/ppermute | solution.py:618
  303.6 13.9 %collective-permute-start.72 = (bf16[256,1024]{1,0:T(8,128)(2,1)}, bf16[256,1024]{1,0:T(8,128)(2,1)}, u32[]{:S(2)}, u32[]{:S(2)}) collective-permute-start(bf16[256,1024]{1,0:T(8,128)(2,1)} %add.299), channel_id=1, source_target_pairs={{0,1},{2,0},{4,2},{6,4},{7,6},{5,7},{3,5},{1,3},{8,9},{10,8},{12,1... | collective-permute-start | bytes 1572872 | tf_op jit(solution)/shard_map/ppermute | solution.py:628
  306.2 13.5 %collective-permute-start.68 = (bf16[256,1024]{1,0:T(8,128)(2,1)}, bf16[256,1024]{1,0:T(8,128)(2,1)}, u32[]{:S(2)}, u32[]{:S(2)}) collective-permute-start(bf16[256,1024]{1,0:T(8,128)(2,1)} %add.295), channel_id=1, source_target_pairs={{0,2},{2,4},{4,6},{6,7},{7,5},{5,3},{3,1},{1,0},{8,10},{10,12},{12... | collective-permute-start | bytes 1572872 | tf_op jit(solution)/shard_map/ppermute | solution.py:628
  308.5 15.4 %all-to-all-start.2 = ((bf16[4,2,128,256]{3,2,1,0:T(8,128)(2,1)}), bf16[4,2,128,256]{3,2,1,0:T(8,128)(2,1)}, u32[]{:S(2)}, u32[]{:S(2)}) async-start(bf16[4,2,128,256]{3,2,1,0:T(8,128)(2,1)} %shard_map.148), calls=%async_computation.2 | async-start | bytes 1048576 | tf_op jit(solution)/shard_map/all_to_all | solution.py:811
  314.7 17.8 %collective-permute-start.59 = (bf16[256,1024]{1,0:T(8,128)(2,1)S(1)}, bf16[256,1024]{1,0:T(8,128)(2,1)}, u32[]{:S(2)}, u32[]{:S(2)}) collective-permute-start(bf16[256,1024]{1,0:T(8,128)(2,1)S(1)} %add_convert_fusion.4.mine), channel_id=1, source_target_pairs={{0,16},{8,24},{16,0},{24,8},{1,17},{9,25},{17,1},{25,9},{2,18},{10... | collective-permute-start | bytes 1572872 | tf_op jit(solution)/shard_map/ppermute | solution.py:618
  337.2 86.8 %collective-permute-start.79 = (bf16[128,1024]{1,0:T(8,128)(2,1)}, bf16[128,1024]{1,0:T(8,128)(2,1)}, u32[]{:S(2)}, u32[]{:S(2)}) collective-permute-start(bf16[128,1024]{1,0:T(8,128)(2,1)} %pad_maximum_fusion.5), channel_id=1, source_target_pairs={{0,1},{2,0},{4,2},{6,4},{7,6},{5,7},{3,5},{1,3},{8,9},{10,8},{12,1... | collective-permute-start | bytes 786440 | tf_op jit(solution)/shard_map/ppermute | solution.py:628
  344.4 81.9 %collective-permute-start.75 = (bf16[128,1024]{1,0:T(8,128)(2,1)}, bf16[128,1024]{1,0:T(8,128)(2,1)}, u32[]{:S(2)}, u32[]{:S(2)}) collective-permute-start(bf16[128,1024]{1,0:T(8,128)(2,1)} %pad_maximum_fusion.4), channel_id=1, source_target_pairs={{0,2},{2,4},{4,6},{6,7},{7,5},{5,3},{3,1},{1,0},{8,10},{10,12},{12... | collective-permute-start | bytes 786440 | tf_op jit(solution)/shard_map/ppermute | solution.py:628
  359.3 13.8 %collective-permute-start.83 = (bf16[256,1024]{1,0:T(8,128)(2,1)}, bf16[256,1024]{1,0:T(8,128)(2,1)}, u32[]{:S(2)}, u32[]{:S(2)}) collective-permute-start(bf16[256,1024]{1,0:T(8,128)(2,1)} %pad_maximum_fusion.2), channel_id=1, source_target_pairs={{0,2},{2,4},{4,6},{6,7},{7,5},{5,3},{3,1},{1,0},{8,10},{10,12},{12... | collective-permute-start | bytes 1572872 | tf_op jit(solution)/shard_map/ppermute | solution.py:628
  371.9 55.1 %collective-permute-start.88 = (bf16[256,1024]{1,0:T(8,128)(2,1)}, bf16[256,1024]{1,0:T(8,128)(2,1)}, u32[]{:S(2)}, u32[]{:S(2)}) collective-permute-start(bf16[256,1024]{1,0:T(8,128)(2,1)} %add.315), channel_id=1, source_target_pairs={{0,1},{2,0},{4,2},{6,4},{7,6},{5,7},{3,5},{1,3},{8,9},{10,8},{12,1... | collective-permute-start | bytes 1572872 | tf_op jit(solution)/shard_map/ppermute | solution.py:628
  384.8 20.4 %collective-permute-start.64 = (bf16[256,1024]{1,0:T(8,128)(2,1)}, bf16[256,1024]{1,0:T(8,128)(2,1)}, u32[]{:S(2)}, u32[]{:S(2)}) collective-permute-start(bf16[256,1024]{1,0:T(8,128)(2,1)} %get-tuple-element.138), channel_id=1, source_target_pairs={{0,8},{8,0},{16,24},{24,16},{1,9},{9,1},{17,25},{25,17},{2,10},{10... | collective-permute-start | bytes 1572872 | tf_op jit(solution)/shard_map/ppermute | solution.py:618
  410.2 17.9 %collective-permute-start.84 = (bf16[256,1024]{1,0:T(8,128)(2,1)}, bf16[256,1024]{1,0:T(8,128)(2,1)}, u32[]{:S(2)}, u32[]{:S(2)}) collective-permute-start(bf16[256,1024]{1,0:T(8,128)(2,1)} %add.311), channel_id=1, source_target_pairs={{0,2},{2,4},{4,6},{6,7},{7,5},{5,3},{3,1},{1,0},{8,10},{10,12},{12... | collective-permute-start | bytes 1572872 | tf_op jit(solution)/shard_map/ppermute | solution.py:628
  424.7 14.4 %collective-permute-start.91 = (bf16[128,1024]{1,0:T(8,128)(2,1)}, bf16[128,1024]{1,0:T(8,128)(2,1)}, u32[]{:S(2)}, u32[]{:S(2)}) collective-permute-start(bf16[128,1024]{1,0:T(8,128)(2,1)} %pad_maximum_fusion.6), channel_id=1, source_target_pairs={{0,2},{2,4},{4,6},{6,7},{7,5},{5,3},{3,1},{1,0},{8,10},{10,12},{12... | collective-permute-start | bytes 786440 | tf_op jit(solution)/shard_map/ppermute | solution.py:628
  426.3 15.4 %collective-permute-start.73 = (bf16[256,1024]{1,0:T(8,128)(2,1)}, bf16[256,1024]{1,0:T(8,128)(2,1)}, u32[]{:S(2)}, u32[]{:S(2)}) collective-permute-start(bf16[256,1024]{1,0:T(8,128)(2,1)} %add.300), channel_id=1, source_target_pairs={{0,1},{2,0},{4,2},{6,4},{7,6},{5,7},{3,5},{1,3},{8,9},{10,8},{12,1... | collective-permute-start | bytes 1572872 | tf_op jit(solution)/shard_map/ppermute | solution.py:628
  427.0 15.1 %collective-permute-start.69 = (bf16[256,1024]{1,0:T(8,128)(2,1)S(1)}, bf16[256,1024]{1,0:T(8,128)(2,1)}, u32[]{:S(2)}, u32[]{:S(2)}) collective-permute-start(bf16[256,1024]{1,0:T(8,128)(2,1)S(1)} %copy-done.157), channel_id=1, source_target_pairs={{0,2},{2,4},{4,6},{6,7},{7,5},{5,3},{3,1},{1,0},{8,10},{10,12},{12... | collective-permute-start | bytes 1572872 | tf_op jit(solution)/shard_map/ppermute | solution.py:628
  440.5 25.6 %collective-permute-start.89 = (bf16[256,1024]{1,0:T(8,128)(2,1)S(1)}, bf16[256,1024]{1,0:T(8,128)(2,1)S(1)}, u32[]{:S(2)}, u32[]{:S(2)}) collective-permute-start(bf16[256,1024]{1,0:T(8,128)(2,1)S(1)} %add.316), channel_id=1, source_target_pairs={{0,1},{2,0},{4,2},{6,4},{7,6},{5,7},{3,5},{1,3},{8,9},{10,8},{12,1... | collective-permute-start | bytes 1572872 | tf_op jit(solution)/shard_map/ppermute | solution.py:628
  441.7 24.7 %collective-permute-start.85 = (bf16[256,1024]{1,0:T(8,128)(2,1)S(1)}, bf16[256,1024]{1,0:T(8,128)(2,1)S(1)}, u32[]{:S(2)}, u32[]{:S(2)}) collective-permute-start(bf16[256,1024]{1,0:T(8,128)(2,1)S(1)} %add.312), channel_id=1, source_target_pairs={{0,2},{2,4},{4,6},{6,7},{7,5},{5,3},{3,1},{1,0},{8,10},{10,12},{12... | collective-permute-start | bytes 1572872 | tf_op jit(solution)/shard_map/ppermute | solution.py:628
  442.1 21.1 %collective-permute-start.96 = (bf16[128,1024]{1,0:T(8,128)(2,1)S(1)}, bf16[128,1024]{1,0:T(8,128)(2,1)S(1)}, u32[]{:S(2)}, u32[]{:S(2)}) collective-permute-start(bf16[128,1024]{1,0:T(8,128)(2,1)S(1)} %add.323), channel_id=1, source_target_pairs={{0,1},{2,0},{4,2},{6,4},{7,6},{5,7},{3,5},{1,3},{8,9},{10,8},{12,1... | collective-permute-start | bytes 786440 | tf_op jit(solution)/shard_map/ppermute | solution.py:628
  446.5 17.9 %collective-permute-start.92 = (bf16[128,1024]{1,0:T(8,128)(2,1)S(1)}, bf16[128,1024]{1,0:T(8,128)(2,1)S(1)}, u32[]{:S(2)}, u32[]{:S(2)}) collective-permute-start(bf16[128,1024]{1,0:T(8,128)(2,1)S(1)} %add.319), channel_id=1, source_target_pairs={{0,2},{2,4},{4,6},{6,7},{7,5},{5,3},{3,1},{1,0},{8,10},{10,12},{12... | collective-permute-start | bytes 786440 | tf_op jit(solution)/shard_map/ppermute | solution.py:628
  447.5 17.3 %collective-permute-start.106 = (f32[1,7,512]{2,1,0:T(8,128)S(1)}, f32[1,7,512]{2,1,0:T(8,128)S(1)}, u32[]{:S(2)}, u32[]{:S(2)}) collective-permute-start(f32[1,7,512]{2,1,0:T(8,128)S(1)} %slice_select_fusion.1), channel_id=1, source_target_pairs={{0,4},{1,5},{2,6},{3,7},{4,0},{5,1},{6,2},{7,3},{8,12},{9,13},{10,... | collective-permute-start | bytes 43016 | tf_op jit(solution)/shard_map/ppermute | solution.py:683
  474.9 14.0 %collective-permute-start.99 = (bf16[128,1024]{1,0:T(8,128)(2,1)S(1)}, bf16[128,1024]{1,0:T(8,128)(2,1)S(1)}, u32[]{:S(2)}, u32[]{:S(2)}) collective-permute-start(bf16[128,1024]{1,0:T(8,128)(2,1)S(1)} %get-tuple-element.211), channel_id=1, source_target_pairs={{0,16},{8,24},{16,0},{24,8},{1,17},{9,25},{17,1},{25,9},{2,18},{10... | collective-permute-start | bytes 786440 | tf_op jit(solution)/shard_map/ppermute | solution.py:618
  477.4 15.0 %collective-permute-start.100 = (bf16[128,1024]{1,0:T(8,128)(2,1)S(1)}, bf16[128,1024]{1,0:T(8,128)(2,1)S(1)}, u32[]{:S(2)}, u32[]{:S(2)}) collective-permute-start(bf16[128,1024]{1,0:T(8,128)(2,1)S(1)} %get-tuple-element.210), channel_id=1, source_target_pairs={{0,24},{8,16},{16,8},{24,0},{1,25},{9,17},{17,9},{25,1},{2,26},{10... | collective-permute-start | bytes 786440 | tf_op jit(solution)/shard_map/ppermute | solution.py:618
  (241 other events, 1773.9 us)
